TPU v7x, 32 devices: a whole 2x2x4 slice. The times are simulated.
32 devices in a mesh: section: 2 (over x), ctx: 4 (over y, core), fsdp: 4 (over z).
Axes of the slice: x: 2, y: 2, z: 4, core: 2. Of those that a mesh axis runs over, the one named last changes fastest.
Arguments:
- ends: bfloat16 [2, 2, 4, 1024, 1152], P('section', None, 'fsdp', 'ctx'), may hold values from -6 to 6
- segment_ids: int32 [2, 4, 1024], P(None, 'fsdp', 'ctx'), may hold values from 0 to 7, never falling along the last dimension, each value on 1 to 512 neighbouring positions
- w_qkv: bfloat16 [2, 1152, 1920], P('section', 'fsdp'), may hold values from -0.1875 to 0.1875
- w_out: bfloat16 [2, 1152, 1152], P('section', 'fsdp'), may hold values from -1 to 1
- w_gate_up: bfloat16 [2, 1152, 6144], P('section', 'fsdp'), may hold values from -0.1875 to 0.1875
- w_down: bfloat16 [2, 3072, 1152], P('section', 'fsdp'), may hold values from -0.109375 to 0.109375
- gains: float32 [2, 2, 1152], P('section'), may hold values from 0.5 to 1.5
Outputs:
- ends_out: float32 [2, 2, 4, 1024, 1152], P('section', None, 'fsdp', 'ctx')
- g_qkv: float32 [2, 1152, 1920], P('section', ('ctx', 'fsdp'))
- g_out: float32 [2, 1152, 1152], P('section', ('ctx', 'fsdp'))
- g_gate_up: float32 [2, 1152, 6144], P('section', ('ctx', 'fsdp'))
- g_down: float32 [2, 3072, 1152], P('section', ('ctx', 'fsdp'))
- g_gains: float32 [2, 2, 1152], P('section', None, ('ctx', 'fsdp'))
Inputs may be any that keep to these rules, and one draw needn't show every extreme that they name: `segment_ids`: within a sequence the ids never fall; every document spans 1 to 512 tokens, and one spans exactly 512.
All inputs are finite; a program needn't handle non-finite values.
Results may differ from a plain program's by a relative error of at most 0.02.
Values may be sent and summed in bfloat16 or wider, within the bound.
A program may use at most 320 MiB of HBM per device.

v0:
```python
import math

import jax
import jax.numpy as jnp
from jax import lax
from jax.experimental import pallas as pl
from jax.experimental.pallas import tpu as pltpu
from jax.sharding import PartitionSpec as P

MESH = pl.DeviceIdType.MESH

D = 1152
HEADS = 18
KV_HEADS = 6
HEAD = 64
FF = 3072
KVW = 384


EPS = 1e-05


def shifted(x, axis, by):
    size = lax.axis_size(axis)
    pairs = [(i, i + by) for i in range(size) if 0 <= i + by < size]
    return lax.ppermute(x, axis, pairs)


def rotate(values_in, cosine, sine_table):
    half_size = values_in.shape[-1] // 2
    front = values_in[..., :half_size]
    back_half = values_in[..., half_size:]
    return jnp.concatenate(
        [front * cosine - back_half * sine_table, back_half * cosine + front * sine_table], axis=-1
    )


def rotate_back(gradient, cosine, sine_table):
    half_size = gradient.shape[-1] // 2
    front = gradient[..., :half_size]
    back_half = gradient[..., half_size:]
    return jnp.concatenate(
        [front * cosine + back_half * sine_table, back_half * cosine - front * sine_table], axis=-1
    )


def norm_forward(inputs, gain_row):
    scale_row = lax.rsqrt(jnp.mean(inputs * inputs, axis=-1, keepdims=True) + EPS)
    unit_rows = inputs * scale_row
    return (unit_rows * gain_row, unit_rows, scale_row)


def norm_backward(gradient, unit_rows, scale_row, gain_row):
    unit_grad = gradient * gain_row
    gain_grad = jnp.sum(gradient * unit_rows, axis=0)
    input_grad = scale_row * (
        unit_grad - unit_rows * jnp.mean(unit_grad * unit_rows, axis=-1, keepdims=True)
    )
    return (input_grad, gain_grad)


def outer_product(left, right):
    return lax.dot_general(
        left, right, (((0,), (0,)), ((), ())), preferred_element_type=jnp.float32
    )


def times_transposed(left, right):
    return lax.dot_general(
        left, right, (((1,), (1,)), ((), ())), preferred_element_type=jnp.float32
    )


def block_needed(first_row, block_rows, seg_full, seg_rows, query_pos):
    last_seg = lax.dynamic_index_in_dim(seg_full, first_row + block_rows - 1, 0, keepdims=False)
    return (first_row <= query_pos[-1]) & (last_seg >= seg_rows[0])


def attend_forward(queries4, key_all, value_all, seg_rows, seg_full, query_pos):
    tok_rows = queries4.shape[0]
    group_size = HEADS // KV_HEADS
    score_scale = HEAD ** (-0.5)
    total_rows = key_all.shape[0]
    block_rows = math.gcd(total_rows, 512)
    block_count = total_rows // block_rows
    key_heads = key_all.reshape(total_rows, KV_HEADS, HEAD)
    value_heads = value_all.reshape(total_rows, KV_HEADS, HEAD)

    def block_scores(block_index):
        first_row = block_index * block_rows
        key_block = lax.dynamic_slice_in_dim(key_heads, first_row, block_rows, 0)
        value_block = lax.dynamic_slice_in_dim(value_heads, first_row, block_rows, 0)
        seg_block = lax.dynamic_slice_in_dim(seg_full, first_row, block_rows, 0)
        key_pos = first_row + jnp.arange(block_rows, dtype=jnp.int32)
        raw_scores = (
            jnp.einsum("qkgd,tkd->kgqt", queries4, key_block, preferred_element_type=jnp.float32)
            * score_scale
        )
        allowed = (key_pos[None, :] <= query_pos[:, None]) & (
            seg_block[None, :] == seg_rows[:, None]
        )
        return (jnp.where(allowed, raw_scores, -1e30), allowed, value_block)

    def first_pass(state_pair, block_index):

        def first_work(state_in):
            row_top, row_total = state_in
            masked, allowed, value_block = block_scores(block_index)
            new_top = jnp.maximum(row_top, jnp.max(masked, axis=-1))
            new_total = row_total * jnp.exp(row_top - new_top) + jnp.sum(
                jnp.exp(masked - new_top[..., None]), axis=-1
            )
            return (new_top, new_total)

        needed = block_needed(block_index * block_rows, block_rows, seg_full, seg_rows, query_pos)
        return (lax.cond(needed, first_work, lambda state_in: state_in, state_pair), None)

    start_state = (
        jnp.full((KV_HEADS, group_size, tok_rows), -1e30, jnp.float32),
        jnp.zeros((KV_HEADS, group_size, tok_rows), jnp.float32),
    )
    block_ids = jnp.arange(block_count, dtype=jnp.int32)
    (row_top, row_total), ignored = lax.scan(first_pass, start_state, block_ids)
    log_total = row_top + jnp.log(row_total)

    def second_pass(summed, block_index):

        def second_work(summed_in):
            masked, allowed, value_block = block_scores(block_index)
            prob_low = jnp.where(allowed, jnp.exp(masked - log_total[..., None]), 0.0).astype(
                jnp.bfloat16
            )
            added = jnp.einsum(
                "kgqt,tkd->qkgd", prob_low, value_block, preferred_element_type=jnp.float32
            )
            return summed_in + added

        needed = block_needed(block_index * block_rows, block_rows, seg_full, seg_rows, query_pos)
        return (lax.cond(needed, second_work, lambda summed_in: summed_in, summed), None)

    start_sum = jnp.zeros((tok_rows, KV_HEADS, group_size, HEAD), jnp.float32)
    attended, ignored = lax.scan(second_pass, start_sum, block_ids)
    return (attended.reshape(tok_rows, D), log_total)


def layer_forward(inputs, weights, gain_pair, seg_rows, seg_full, query_pos, cosine, sine_table):
    w_qkv, w_out, w_gate_up, w_down = weights
    tok_rows = inputs.shape[0]
    group_size = HEADS // KV_HEADS
    normed, unit_one, scale_one = norm_forward(inputs, gain_pair[0])
    normed_low = normed.astype(jnp.bfloat16)
    mixed_proj = jnp.dot(normed_low, w_qkv, preferred_element_type=jnp.float32)
    queries = rotate(mixed_proj[:, :D].reshape(tok_rows, HEADS, HEAD), cosine, sine_table).astype(
        jnp.bfloat16
    )
    key_rows = rotate(
        mixed_proj[:, D : D + KVW].reshape(tok_rows, KV_HEADS, HEAD), cosine, sine_table
    )
    key_rows = key_rows.astype(jnp.bfloat16).reshape(tok_rows, KVW)
    value_rows = mixed_proj[:, D + KVW :].astype(jnp.bfloat16)
    key_all, value_all = (
        lax.all_gather(key_rows, "ctx", axis=0, tiled=True),
        lax.all_gather(value_rows, "ctx", axis=0, tiled=True),
    )
    queries4 = queries.reshape(tok_rows, KV_HEADS, group_size, HEAD)
    attended, log_total = attend_forward(
        queries4, key_all, value_all, seg_rows, seg_full, query_pos
    )
    context = attended.astype(jnp.bfloat16)
    hidden = inputs + jnp.dot(context, w_out, preferred_element_type=jnp.float32)
    second, unit_two, scale_two = norm_forward(hidden, gain_pair[1])
    second_low = second.astype(jnp.bfloat16)
    gate_up = jnp.dot(second_low, w_gate_up, preferred_element_type=jnp.float32)
    gate_pre = gate_up[:, :FF]
    up_pre = gate_up[:, FF:]
    inner_act = (jax.nn.silu(gate_pre) * up_pre).astype(jnp.bfloat16)
    result = hidden + jnp.dot(inner_act, w_down, preferred_element_type=jnp.float32)
    saved_acts = (
        normed_low,
        queries4,
        key_all,
        value_all,
        attended,
        log_total,
        context,
        unit_one,
        scale_one,
        unit_two,
        scale_two,
        second_low,
        gate_pre,
        up_pre,
        inner_act,
    )
    return (result, saved_acts)


def layer_backward(
    grad_low, saved_acts, weights, gain_pair, seg_rows, seg_full, query_pos, cosine, sine_table
):
    w_qkv, w_out, w_gate_up, w_down = weights
    (
        normed_low,
        queries4,
        key_all,
        value_all,
        attended,
        log_total,
        context,
        unit_one,
        scale_one,
        unit_two,
        scale_two,
        second_low,
        gate_pre,
        up_pre,
        inner_act,
    ) = saved_acts
    tok_rows = grad_low.shape[0]
    group_size = HEADS // KV_HEADS
    score_scale = HEAD ** (-0.5)
    grad_out = grad_low.astype(jnp.float32)
    grad_inner = times_transposed(grad_low, w_down)
    sigmoid_gate = jax.nn.sigmoid(gate_pre)
    silu_gate = gate_pre * sigmoid_gate
    grad_gate = grad_inner * up_pre * sigmoid_gate * (1.0 + gate_pre * (1.0 - sigmoid_gate))
    grad_up = grad_inner * silu_gate
    grad_both = jnp.concatenate([grad_gate, grad_up], axis=1).astype(jnp.bfloat16)
    grad_second = times_transposed(grad_both, w_gate_up)
    grad_norm_two, gain_two = norm_backward(grad_second, unit_two, scale_two, gain_pair[1])
    grad_hidden = grad_out + grad_norm_two
    hidden_low = grad_hidden.astype(jnp.bfloat16)
    grad_context = times_transposed(hidden_low, w_out).astype(jnp.bfloat16)
    grad_context4 = grad_context.reshape(tok_rows, KV_HEADS, group_size, HEAD)
    attended4 = attended.reshape(tok_rows, KV_HEADS, group_size, HEAD)
    row_delta = jnp.einsum("qkgd,qkgd->kgq", grad_context4.astype(jnp.float32), attended4)
    total_rows = seg_full.shape[0]
    start_state = (
        jnp.zeros((tok_rows, KV_HEADS, group_size, HEAD), jnp.float32),
        jnp.zeros((total_rows, 2 * KVW), jnp.float32),
    )
    key_piece, value_piece = key_all, value_all
    piece_rows = key_piece.shape[0]
    block_rows = math.gcd(piece_rows, 512)
    block_count = piece_rows // block_rows

    def one_block(block_index, inner_state):
        offset = block_index * block_rows

        def one_work(state_in):
            grad_query, grad_kv = state_in
            key_block = lax.dynamic_slice_in_dim(key_piece, offset, block_rows, 0).reshape(
                block_rows, KV_HEADS, HEAD
            )
            value_block = lax.dynamic_slice_in_dim(value_piece, offset, block_rows, 0).reshape(
                block_rows, KV_HEADS, HEAD
            )
            seg_block = lax.dynamic_slice_in_dim(seg_full, offset, block_rows, 0)
            key_pos = offset + jnp.arange(block_rows, dtype=jnp.int32)
            raw_scores = (
                jnp.einsum(
                    "qkgd,tkd->kgqt", queries4, key_block, preferred_element_type=jnp.float32
                )
                * score_scale
            )
            allowed = (key_pos[None, :] <= query_pos[:, None]) & (
                seg_block[None, :] == seg_rows[:, None]
            )
            prob_full = jnp.where(allowed, jnp.exp(raw_scores - log_total[..., None]), 0.0)
            prob_low = prob_full.astype(jnp.bfloat16)
            grad_value = jnp.einsum(
                "kgqt,qkgd->tkd", prob_low, grad_context4, preferred_element_type=jnp.float32
            )
            grad_prob = jnp.einsum(
                "qkgd,tkd->kgqt", grad_context4, value_block, preferred_element_type=jnp.float32
            )
            grad_scores = (prob_full * (grad_prob - row_delta[..., None])).astype(jnp.bfloat16)
            grad_query = (
                grad_query
                + jnp.einsum(
                    "kgqt,tkd->qkgd", grad_scores, key_block, preferred_element_type=jnp.float32
                )
                * score_scale
            )
            grad_key = (
                jnp.einsum(
                    "kgqt,qkgd->tkd", grad_scores, queries4, preferred_element_type=jnp.float32
                )
                * score_scale
            )
            new_rows = jnp.concatenate(
                [grad_key.reshape(block_rows, KVW), grad_value.reshape(block_rows, KVW)], axis=1
            )
            old_rows = lax.dynamic_slice_in_dim(grad_kv, offset, block_rows, 0)
            grad_kv = lax.dynamic_update_slice_in_dim(grad_kv, old_rows + new_rows, offset, 0)
            return (grad_query, grad_kv)

        needed = block_needed(offset, block_rows, seg_full, seg_rows, query_pos)
        return lax.cond(needed, one_work, lambda state_in: state_in, inner_state)

    grad_query, grad_kv_all = lax.fori_loop(0, block_count, one_block, start_state)
    grad_kv_own = lax.psum_scatter(
        grad_kv_all.astype(jnp.bfloat16), "ctx", scatter_dimension=0, tiled=True
    ).astype(jnp.float32)
    grad_q_pre = rotate_back(grad_query.reshape(tok_rows, HEADS, HEAD), cosine, sine_table).reshape(
        tok_rows, D
    )
    grad_k_pre = rotate_back(
        grad_kv_own[:, :KVW].reshape(tok_rows, KV_HEADS, HEAD), cosine, sine_table
    ).reshape(tok_rows, KVW)
    grad_mixed = jnp.concatenate([grad_q_pre, grad_k_pre, grad_kv_own[:, KVW:]], axis=1).astype(
        jnp.bfloat16
    )
    grad_normed = times_transposed(grad_mixed, w_qkv)
    grad_norm_one, gain_one = norm_backward(grad_normed, unit_one, scale_one, gain_pair[0])
    grad_input = grad_hidden + grad_norm_one
    operand_pairs = (
        normed_low,
        context,
        second_low,
        inner_act,
        grad_mixed,
        hidden_low,
        grad_both,
        grad_low,
    )
    return (grad_input, operand_pairs, jnp.stack([gain_one, gain_two]))


def gather_kernel(qo, gu, dn, fqo, fgu, fdn, own_sem, back_sem, zs, zr, ys, yr, cs, cr, es, er):
    place = lax.axis_index("ctx")
    z = lax.axis_index("fsdp")
    last = lax.axis_size("fsdp") - 1
    y, k = place // 2, place % 2
    y_mate = {"ctx": (1 - y) * 2 + k}
    k_mate = {"ctx": y * 2 + 1 - k}
    width = qo.shape[0]
    deep = dn.shape[0]
    half = width // 2
    chunks = [(0, p) for p in range(3)] + [(1, p) for p in range(3)] + [(2, p) for p in range(2)]
    wholes = (fqo, fgu, fdn)
    owns = (qo, gu, dn)

    def view(refs, shard, yy, kk, chunk):
        m, p = chunk
        ref = refs[m]
        if m == 2:
            rows = deep // 8
            first = shard * deep + (yy * 2 + kk) * (deep // 4) + p * rows
            return ref.at[pl.ds(pl.multiple_of(first, 16), rows), :]
        rows = half // 3
        cols = ref.shape[1] // 2
        first = shard * width + yy * half + p * rows
        return ref.at[pl.ds(pl.multiple_of(first, 16), rows), pl.ds(pl.multiple_of(kk * cols, 128), cols)]

    barrier = pltpu.get_barrier_semaphore()
    for mate in (y_mate, k_mate):
        pl.semaphore_signal(barrier, inc=1, device_id=mate, device_id_type=MESH)

    @pl.when(z > 0)
    def _():
        pl.semaphore_signal(barrier, inc=1, device_id={"fsdp": z - 1}, device_id_type=MESH)

    @pl.when(z < last)
    def _():
        pl.semaphore_signal(barrier, inc=1, device_id={"fsdp": z + 1}, device_id_type=MESH)

    pl.semaphore_wait(barrier, 2 + jnp.where(z > 0, 1, 0) + jnp.where(z < last, 1, 0))

    def z_copy(shard, j, to, first, back):
        chunk = chunks[j]
        src = view(owns, 0, y, k, chunk) if first else view(wholes, shard, y, k, chunk)
        return pltpu.make_async_remote_copy(
            src_ref=src, dst_ref=view(wholes, shard, y, k, chunk),
            send_sem=back_sem.at[j] if back else zs.at[shard, j], recv_sem=zr.at[shard, j],
            device_id={"fsdp": to}, device_id_type=MESH)

    def mate_copy(shard, j, yy, mate, send, recv):
        chunk = chunks[j]
        ref = view(wholes, shard, yy, k, chunk)
        return pltpu.make_async_remote_copy(
            src_ref=ref, dst_ref=ref, send_sem=send.at[shard, j], recv_sem=recv.at[shard, j],
            device_id=mate, device_id_type=MESH)

    def arrive(shard, j, yy, kk, recv):
        ref = view(wholes, shard, yy, kk, chunks[j])
        pltpu.make_async_remote_copy(
            src_ref=ref, dst_ref=ref, send_sem=recv.at[shard, j], recv_sem=recv.at[shard, j],
            device_id=k_mate, device_id_type=MESH).wait_recv()

    for j in range(len(chunks)):
        @pl.when(z < last)
        def _():
            z_copy(z, j, z + 1, True, False).start()

        @pl.when(z > 0)
        def _():
            z_copy(z, j, z - 1, True, True).start()
    locals_ = []
    for m in range(3):
        rows = owns[m].shape[0]
        locals_.append(pltpu.make_async_remote_copy(
            src_ref=owns[m], dst_ref=wholes[m].at[pl.ds(pl.multiple_of(z * rows, 16), rows), :],
            send_sem=own_sem.at[0, m], recv_sem=own_sem.at[1, m], device_id=k_mate, device_id_type=MESH))
    for copy in locals_:
        copy.start()

    def sides(d):
        return ((z - d >= 0, z - d, z + 1, z < last), (z + d <= last, z + d, z - 1, z > 0))

    def relay(d, j):
        for valid, shard, onward, more in sides(d):
            @pl.when(valid)
            def _():
                arrive(shard, j, y, k, zr)
                if d < 3:
                    @pl.when(more)
                    def _():
                        z_copy(shard, j, onward, False, False).start()
                mate_copy(shard, j, y, y_mate, ys, yr).start()
                mate_copy(shard, j, y, k_mate, cs, cr).start()

    def across(d, j):
        for valid, shard, onward, more in sides(d):
            @pl.when(valid)
            def _():
                arrive(shard, j, 1 - y, k, yr)
                mate_copy(shard, j, 1 - y, k_mate, es, er).start()

    order = [(d, j) for d in (1, 2, 3) for j in range(len(chunks))]
    lag = 1
    for i, (d, j) in enumerate(order):
        relay(d, j)
        if i >= lag:
            across(*order[i - lag])
    for d, j in order[len(order) - lag:]:
        across(d, j)
    for d, j in order:
        for valid, shard, onward, more in sides(d):
            @pl.when(valid)
            def _():
                arrive(shard, j, y, 1 - k, cr)
                arrive(shard, j, 1 - y, 1 - k, er)
                mate_copy(shard, j, y, y_mate, ys, yr).wait_send()
                mate_copy(shard, j, y, k_mate, cs, cr).wait_send()
                mate_copy(shard, j, 1 - y, k_mate, es, er).wait_send()
                if d < 3:
                    @pl.when(more)
                    def _():
                        z_copy(shard, j, onward, False, False).wait_send()
    for j in range(len(chunks)):
        @pl.when(z < last)
        def _():
            z_copy(z, j, z + 1, True, False).wait_send()

        @pl.when(z > 0)
        def _():
            z_copy(z, j, z - 1, True, True).wait_send()
    for copy in locals_:
        copy.wait()


def gather_weights(qo, gu, dn):
    size = lax.axis_size("fsdp")
    any_spec = pl.BlockSpec(memory_space=pl.ANY)
    return pl.pallas_call(
        gather_kernel,
        out_shape=tuple(jax.ShapeDtypeStruct((size * w.shape[0], w.shape[1]), w.dtype) for w in (qo, gu, dn)),
        in_specs=[any_spec] * 3,
        out_specs=(any_spec,) * 3,
        scratch_shapes=[pltpu.SemaphoreType.DMA((2, 3)), pltpu.SemaphoreType.DMA((8,))]
        + [pltpu.SemaphoreType.DMA((4, 8))] * 8,
        compiler_params=pltpu.CompilerParams(collective_id=1, has_side_effects=True),
        name="weights_gather",
    )(qo, gu, dn)


DOWN_COLS = 128
WIDE_COLS = 384
NEAR, MID, FAR, SUMS = 2, 4, 8, 12


def reduce_kernel(
    inner_h, grad_h, second_h, both_h, normed_h, mixed_h, context_h, hidden_h, gain_tiles,
    o_down, o_gate_up, o_qkv, o_out, o_gain,
    *scratch,
):
    kinds = (scratch[0:9], scratch[9:18])
    (near_send, near_recv, mid_send, mid_recv, right_send, right_recv, left_send, left_recv,
     near_free, mid_free, right_free, left_free) = scratch[18:30]
    operands, load_sem, gain_in, gain_send, gain_recv = scratch[30:38], *scratch[38:42]
    inner_t, g_low, second_t, both, normed_t, mixed, context_t, hidden_low = operands
    loads = [
        pltpu.make_async_copy(src, dst, load_sem.at[i])
        for i, (src, dst) in enumerate(
            zip((inner_h, grad_h, second_h, both_h, normed_h, mixed_h, context_h, hidden_h), operands)
        )
    ]
    for load in loads:
        load.start()
    place = lax.axis_index("ctx")
    z = lax.axis_index("fsdp")
    last = lax.axis_size("fsdp") - 1
    y, k = place // 2, place % 2
    y_mate = {"ctx": (1 - y) * 2 + k}
    k_mate = {"ctx": y * 2 + 1 - k}
    right, left = {"fsdp": z + 1}, {"fsdp": z - 1}
    f32, low = jnp.float32, jnp.bfloat16

    n_down = g_low.shape[0] // DOWN_COLS
    n_both = both.shape[0] // WIDE_COLS
    n_mixed = mixed.shape[0] // WIDE_COLS
    n_out = hidden_low.shape[0] // WIDE_COLS
    end_both = n_down + n_both
    end_mixed = end_both + n_mixed
    total = end_mixed + n_out
    hop = 2
    first_z = 3
    final_lag = first_z + hop * 3

    barrier = pltpu.get_barrier_semaphore()
    me = place * 4 + z
    others = [((place + i // 4) % 4, (z + i % 4) % 4) for i in range(1, 16)]
    for to_place, to_z in others:
        pl.semaphore_signal(barrier, inc=1, device_id={"ctx": to_place, "fsdp": to_z}, device_id_type=MESH)
    pl.semaphore_wait(barrier, 15)

    def gain_copy(i):
        to_place, to_z = others[i - 1]
        return pltpu.make_async_remote_copy(
            src_ref=gain_tiles.at[to_place * 4 + to_z], dst_ref=gain_in.at[i],
            send_sem=gain_send.at[i], recv_sem=gain_recv.at[i],
            device_id={"ctx": to_place, "fsdp": to_z}, device_id_type=MESH)

    for i in range(1, 16):
        gain_copy(i).start()

    def typed(j, work):
        @pl.when((j >= 0) & (j < n_down))
        def _():
            work(0)

        @pl.when((j >= n_down) & (j < total))
        def _():
            work(1)

    def near_copy(kind, j):
        out_near, own_near, in_near = kinds[kind][0:3]
        slot = j % NEAR
        return pltpu.make_async_remote_copy(
            src_ref=out_near.at[slot], dst_ref=in_near.at[slot], send_sem=near_send.at[slot],
            recv_sem=near_recv.at[slot], device_id=k_mate, device_id_type=MESH)

    def mid_copy(kind, j):
        out_mid, in_mid = kinds[kind][3:5]
        slot = j % MID
        return pltpu.make_async_remote_copy(
            src_ref=out_mid.at[slot], dst_ref=in_mid.at[slot], send_sem=mid_send.at[slot],
            recv_sem=mid_recv.at[slot], device_id=y_mate, device_id_type=MESH)

    def line_rows(kind, step, rightward):
        rows = kinds[kind][5].shape[1]
        part = rows // 4
        if rightward:
            start = (part * (step + 1)) // 16 * 16
            return start, rows - start
        return 0, (part * step + 15) // 16 * 16

    def line_copy(kind, j, step, rightward):
        start, count = line_rows(kind, step, rightward)
        src, dst = (kinds[kind][6], kinds[kind][7]) if rightward else (kinds[kind][6], kinds[kind][8])
        lane = 0 if rightward else 1
        return pltpu.make_async_remote_copy(
            src_ref=src.at[lane, j % NEAR, pl.ds(start, count), :],
            dst_ref=dst.at[j % FAR, pl.ds(start, count), :],
            send_sem=(right_send if rightward else left_send).at[j % NEAR],
            recv_sem=(right_recv if rightward else left_recv).at[j % FAR],
            device_id=right if rightward else left, device_id_type=MESH)

    def multiply(kind, j, lhs, rhs, first, cols):
        out_near, own_near = kinds[kind][0:2]
        slot = j % NEAR
        rows = own_near.shape[2]
        columns = pl.ds(pl.multiple_of((j - first) * cols, 128), cols)
        block = rhs[columns, :]
        for yy in range(2):
            for mine in (False, True):
                kk = k if mine else 1 - k
                at = pl.ds(pl.multiple_of((yy * 2 + kk) * rows, 16), rows)
                part = lax.dot_general(lhs[at, :], block, (((1,), (1,)), ((), ())), preferred_element_type=f32)
                (own_near if mine else out_near)[slot, yy] = part.astype(low)

    def stage_near(j):
        for i, first in enumerate((0, n_down, end_both, end_mixed)):
            @pl.when(j == first)
            def _(i=i):
                loads[2 * i].wait()
                loads[2 * i + 1].wait()

        @pl.when((j >= NEAR) & (j < total))
        def _():
            typed(j - NEAR, lambda kind: near_copy(kind, j - NEAR).wait_send())

        @pl.when(j < n_down)
        def _():
            multiply(0, j, inner_t, g_low, 0, DOWN_COLS)

        @pl.when((j >= n_down) & (j < end_both))
        def _():
            multiply(1, j, second_t, both, n_down, WIDE_COLS)

        @pl.when((j >= end_both) & (j < end_mixed))
        def _():
            multiply(1, j, normed_t, mixed, end_both, WIDE_COLS)

        @pl.when((j >= end_mixed) & (j < total))
        def _():
            multiply(1, j, context_t, hidden_low, end_mixed, WIDE_COLS)

        @pl.when((j >= NEAR) & (j < total))
        def _():
            pl.semaphore_wait(near_free, 1)

        typed(j, lambda kind: near_copy(kind, j).start())

    def stage_mid(j):
        def work(kind):
            out_near, own_near, in_near, out_mid, in_mid, sums = kinds[kind][0:6]
            near_copy(kind, j).wait_recv()
            slot = j % NEAR
            out_mid[j % MID] = (own_near[slot, 1 - y].astype(f32) + in_near[slot, 1 - y].astype(f32)).astype(low)
            sums[j % SUMS] = own_near[slot, y].astype(f32) + in_near[slot, y].astype(f32)

        @pl.when((j >= MID) & (j < total))
        def _():
            typed(j - MID, lambda kind: mid_copy(kind, j - MID).wait_send())

        typed(j, work)

        @pl.when((j >= 0) & (j + NEAR < total))
        def _():
            pl.semaphore_signal(near_free, inc=1, device_id=k_mate, device_id_type=MESH)

        @pl.when((j >= MID) & (j < total))
        def _():
            pl.semaphore_wait(mid_free, 1)

        typed(j, lambda kind: mid_copy(kind, j).start())

    def stage_sum(j):
        def work(kind):
            in_mid, sums = kinds[kind][4:6]
            mid_copy(kind, j).wait_recv()
            sums[j % SUMS] = sums[j % SUMS] + in_mid[j % MID].astype(f32)

        typed(j, work)

        @pl.when((j >= 0) & (j + MID < total))
        def _():
            pl.semaphore_signal(mid_free, inc=1, device_id=y_mate, device_id_type=MESH)

    def stage_line(i, rightward):
        free = right_free if rightward else left_free
        for at in range(4):
            step = at if rightward else 3 - at
            if step == 3:
                continue
            j = i - first_z - hop * step

            @pl.when((z == at) & (j >= 0) & (j < total))
            def _(at=at, step=step, j=j):
                @pl.when(j >= NEAR)
                def _():
                    typed(j - NEAR, lambda kind: line_copy(kind, j - NEAR, at, rightward).wait_send())

                def work(kind):
                    sums, out_line, in_right, in_left = kinds[kind][5:9]
                    start, count = line_rows(kind, at, rightward)
                    rows = pl.ds(start, count)
                    value = sums[j % SUMS, rows, :]
                    if step > 0:
                        came = line_rows(kind, at - 1 if rightward else at + 1, rightward)
                        arrive = line_copy(kind, j, at - 1 if rightward else at + 1, rightward)
                        arrive.wait_recv()
                        value = value + (in_right if rightward else in_left)[j % FAR, rows, :].astype(f32)
                    out_line[0 if rightward else 1, j % NEAR, rows, :] = value.astype(low)

                typed(j, work)

                @pl.when(j >= FAR)
                def _():
                    pl.semaphore_wait(free, 1)

                typed(j, lambda kind: line_copy(kind, j, at, rightward).start())

    def store(kind, j, value):
        if kind == 0:
            o_down[:, pl.ds(pl.multiple_of(j * DOWN_COLS, 128), DOWN_COLS)] = value
            return
        for out, first, end in ((o_gate_up, n_down, end_both), (o_qkv, end_both, end_mixed), (o_out, end_mixed, total)):
            @pl.when((j >= first) & (j < end))
            def _(out=out, first=first):
                out[:, pl.ds(pl.multiple_of((j - first) * WIDE_COLS, 128), WIDE_COLS)] = value

    def stage_final(j):
        for at in range(4):
            @pl.when((z == at) & (j >= 0) & (j < total))
            def _(at=at):
                def work(kind):
                    sums, out_line, in_right, in_left = kinds[kind][5:9]
                    part = sums.shape[1] // 4
                    if at == 3:
                        line_copy(kind, j, 2, True).wait_recv()
                    if at == 0:
                        line_copy(kind, j, 1, False).wait_recv()
                    low_at = at * part // 16 * 16
                    high_at = (at * part + part + 15) // 16 * 16
                    rows = pl.ds(low_at, high_at - low_at)
                    value = sums[j % SUMS, rows, :]
                    if at > 0:
                        value = value + in_right[j % FAR, rows, :].astype(f32)
                    if at < 3:
                        value = value + in_left[j % FAR, rows, :].astype(f32)
                    shift = at * part - low_at
                    store(kind, j, value[shift:shift + part])

                typed(j, work)
                if at > 0:
                    @pl.when(j + FAR < total)
                    def _():
                        pl.semaphore_signal(right_free, inc=1, device_id=left, device_id_type=MESH)
                if at < 3:
                    @pl.when(j + FAR < total)
                    def _():
                        pl.semaphore_signal(left_free, inc=1, device_id=right, device_id_type=MESH)

    def iteration(i, carry):
        stage_near(i)
        stage_mid(i - 1)
        stage_sum(i - 3)
        stage_line(i, True)
        stage_line(i, False)
        stage_final(i - final_lag)
        return carry

    lax.fori_loop(0, total + final_lag, iteration, 0)
    gain = gain_tiles[me]
    for i in range(1, 16):
        gain_copy(i).wait()
        gain = gain + gain_in[i]
    o_gain[...] = gain
    for j in range(total - NEAR, total):
        near_copy(1, j).wait_send()
        for at in range(3):
            @pl.when(z == at)
            def _(at=at):
                line_copy(1, j, at, True).wait_send()

            @pl.when(z == at + 1)
            def _(at=at):
                line_copy(1, j, at + 1, False).wait_send()
    for j in range(total - MID, total):
        mid_copy(1, j).wait_send()


def reduce_grads(lefts, rights, gain_tiles):
    normed, context, second, inner = lefts
    both, mixed, hidden, grad = rights
    ops = (inner, grad, second, both, normed, mixed, context, hidden)
    low, f32 = jnp.bfloat16, jnp.float32
    scratch = []
    for rows, cols in ((inner.shape[0] // 4, DOWN_COLS), (second.shape[0] // 4, WIDE_COLS)):
        scratch += [
            pltpu.VMEM((NEAR, 2, rows, cols), low), pltpu.VMEM((NEAR, 2, rows, cols), low), pltpu.VMEM((NEAR, 2, rows, cols), low),
            pltpu.VMEM((MID, rows, cols), low), pltpu.VMEM((MID, rows, cols), low),
            pltpu.VMEM((SUMS, rows, cols), f32),
            pltpu.VMEM((2, NEAR, rows, cols), low),
            pltpu.VMEM((FAR, rows, cols), low), pltpu.VMEM((FAR, rows, cols), low)]
    sem = pltpu.SemaphoreType
    scratch += [sem.DMA((NEAR,)), sem.DMA((NEAR,)), sem.DMA((MID,)), sem.DMA((MID,)),
                sem.DMA((NEAR,)), sem.DMA((FAR,)), sem.DMA((NEAR,)), sem.DMA((FAR,)),
                sem.REGULAR, sem.REGULAR, sem.REGULAR, sem.REGULAR]
    scratch += [pltpu.VMEM(op.shape, low) for op in ops]
    scratch += [sem.DMA((8,)), pltpu.VMEM((16, 8, 128), f32), sem.DMA((16,)), sem.DMA((16,))]
    outs = [(a.shape[0] // 16, b.shape[0]) for a, b in zip(ops[0::2], ops[1::2])] + [(8, 128)]
    vm, hbm = pl.BlockSpec(memory_space=pltpu.VMEM), pl.BlockSpec(memory_space=pl.ANY)
    return pl.pallas_call(
        reduce_kernel,
        out_shape=tuple(jax.ShapeDtypeStruct(s, f32) for s in outs),
        in_specs=[hbm] * 8 + [vm],
        out_specs=(vm,) * 5,
        scratch_shapes=scratch,
        compiler_params=pltpu.CompilerParams(collective_id=2, has_side_effects=True, vmem_limit_bytes=62 * 2**20),
        name="grads_reduce",
    )(*ops, gain_tiles)


F32, LOW = jnp.float32, jnp.bfloat16
GROUP = HEADS // KV_HEADS
HALF = HEAD // 2
SCALE = HEAD ** (-0.5)
NONE = -1e30
TILE = 384
WIDE = 512


def dot(left, right, left_dim, right_dim):
    return lax.dot_general(
        left, right, (((left_dim,), (right_dim,)), ((), ())), preferred_element_type=F32
    )


def at(start, size, step=128):
    return pl.ds(pl.multiple_of(start, step), size)


def column_scale(v):
    return lax.rsqrt(jnp.mean(v * v, axis=0, keepdims=True) + EPS)


def greet(peers):
    barrier = pltpu.get_barrier_semaphore()
    for peer in peers:
        pl.semaphore_signal(barrier, inc=1, device_id=peer, device_id_type=MESH)
    pl.semaphore_wait(barrier, len(peers))


def remote(src, dst, send, recv, peer):
    return pltpu.make_async_remote_copy(
        src_ref=src, dst_ref=dst, send_sem=send, recv_sem=recv, device_id=peer, device_id_type=MESH
    )


def fill_bias(bias, seg_row, seg_col, m, place, toks):
    own = seg_row[m]
    rows = lax.broadcasted_iota(jnp.int32, (toks, toks), 0)
    cols = lax.broadcasted_iota(jnp.int32, (toks, toks), 1)
    for d in range(3):
        first = jnp.maximum(place - d, 0) * toks
        keys = seg_col[m, pl.ds(pl.multiple_of(first, 128), toks), :]
        allowed = keys == own
        if d == 0:
            allowed = allowed & (rows <= cols)
        bias[d] = jnp.where(allowed, 0.0, NONE)


def forward_kernel(
    ends, gains, cosine, sine, seg_row, seg_col, w_joint, w_gate_up, w_down,
    o_normed, o_context, o_second, o_inner, o_x, o_q, o_kv, o_att, o_lse, o_hidden, o_gu, o_result,
    v_joint, v_gate_up, v_down, x_in, x_now, s_normed, s_context, s_second, s_inner, s_x,
    s_q, s_kv, s_att, s_top, s_lse, s_hidden, s_gu, s_result, bias,
    w_sem, save_sem, kv_send, kv_recv, x_send, x_recv,
):
    section = lax.axis_index("section")
    place = lax.axis_index("ctx")
    micros, toks = ends.shape[0], ends.shape[1]
    qkv = D + 2 * KVW
    loads = [
        pltpu.make_async_copy(src, dst, w_sem.at[i])
        for i, (src, dst) in enumerate(
            ((w_joint, v_joint), (w_gate_up, v_gate_up), (w_down, v_down))
        )
    ]
    for load in loads:
        load.start()
    greet([{"ctx": (place + i) % 4} for i in (1, 2, 3)] + [{"section": 1 - section}])

    def saves(m):
        lanes = at(m * toks, toks)
        pairs = (
            (s_normed, o_normed.at[:, lanes]),
            (s_context, o_context.at[:, lanes]),
            (s_second, o_second.at[:, lanes]),
            (s_inner, o_inner.at[:, lanes]),
            (s_x, o_x.at[m]),
            (s_q, o_q.at[m]),
            (s_kv.at[m], o_kv.at[m]),
            (s_att, o_att.at[m]),
            (s_lse, o_lse.at[m]),
            (s_hidden, o_hidden.at[m]),
            (s_gu, o_gu.at[m]),
        )
        return [pltpu.make_async_copy(a, b, save_sem.at[i]) for i, (a, b) in enumerate(pairs)]

    def result_save(m):
        return pltpu.make_async_copy(s_result, o_result.at[m], save_sem.at[11])

    def x_copy(m):
        return remote(x_in.at[m], x_in.at[m], x_send.at[m], x_recv.at[m], {"section": 1})

    def kv_copy(m, source, slot, lane, to):
        return remote(
            s_kv.at[m, source], s_kv.at[m, slot], kv_send.at[m, lane], kv_recv.at[m, slot],
            {"ctx": to},
        )

    def kv_sends(m):
        return (
            (0, kv_copy(m, 0, 1, 0, 1)),
            (0, kv_copy(m, 0, 2, 1, 2)),
            (1, kv_copy(m, 0, 2, 0, 3)),
            (2, kv_copy(m, 0, 1, 0, 3)),
        )

    def attend(kv_at, m, blocks, fresh):
        rows = at(kv_at * HEAD, HEAD, 64)
        query = s_q[rows, :]
        parts = []
        for d in blocks:
            part = dot(s_kv[m, d, rows, :], query, 0, 0)
            mask = bias[d]
            parts.append(part + jnp.concatenate([mask] * GROUP, axis=1))
        scores = parts[0] if len(parts) == 1 else jnp.concatenate(parts, axis=0)
        top = jnp.max(scores, axis=0, keepdims=True)
        one = pl.ds(kv_at, 1)
        if not fresh:
            old_top, old_total = s_top[one, :], s_lse[one, :]
            top = jnp.maximum(top, old_top)
        probs = jnp.exp(scores - top)
        total = jnp.sum(probs, axis=0, keepdims=True)
        probs = probs.astype(LOW)
        value_rows = at(KVW + kv_at * HEAD, HEAD, 64)
        summed = None
        for i, d in enumerate(blocks):
            term = dot(s_kv[m, d, value_rows, :], probs[i * toks : (i + 1) * toks], 1, 0)
            summed = term if summed is None else summed + term
        if not fresh:
            keep = jnp.exp(old_top - top)
            total = total + old_total * keep
        s_top[one, :] = top
        s_lse[one, :] = total
        for g in range(GROUP):
            lanes = slice(g * toks, (g + 1) * toks)
            out_rows = at((kv_at * GROUP + g) * HEAD, HEAD, 64)
            value = summed[:, lanes]
            if not fresh:
                value = value + s_att[out_rows, :] * keep[:, lanes]
            s_att[out_rows, :] = value

    def micro(m, carry):
        @pl.when(m > 0)
        def _():
            for save in saves(m - 1):
                save.wait()

            @pl.when(section == 1)
            def _():
                result_save(m - 1).wait()

        @pl.when(section == 0)
        def _():
            x_now[...] = ends[m].astype(F32).T

        @pl.when(section == 1)
        def _():
            x_copy(m).wait_recv()
            x_now[...] = x_in[m].astype(F32)

        fill_bias(bias, seg_row, seg_col, m, place, toks)
        x = x_now[...]
        s_x[...] = x.astype(LOW)
        s_normed[...] = (x * column_scale(x) * gains[:, 0:1]).astype(LOW)

        @pl.when(m == 0)
        def _():
            loads[0].wait()

        cos, sin = cosine[...], sine[...]

        def rotated(block, head):
            front = block[head * HEAD : head * HEAD + HALF]
            back = block[head * HEAD + HALF : (head + 1) * HEAD]
            return jnp.concatenate([front * cos - back * sin, back * cos + front * sin], axis=0)

        keys = dot(v_joint[:, D : D + KVW], s_normed[...], 0, 0)
        for head in range(KV_HEADS):
            s_kv[m, 0, head * HEAD : (head + 1) * HEAD, :] = rotated(keys, head).astype(LOW)
        s_kv[m, 0, KVW : 2 * KVW, :] = dot(
            v_joint[:, D + KVW : qkv], s_normed[...], 0, 0
        ).astype(LOW)
        for who, copy in kv_sends(m):
            @pl.when(place == who)
            def _(copy=copy):
                copy.start()

        def query_tile(i, carry):
            block = dot(v_joint[:, at(i * TILE, TILE)], s_normed[...], 0, 0) * SCALE
            for head in range(TILE // HEAD):
                rows = at((i * (TILE // HEAD // GROUP) + head // GROUP) * HEAD, HEAD, 64)
                g = head % GROUP
                s_q[rows, g * toks : (g + 1) * toks] = rotated(block, head).astype(LOW)
            return carry

        lax.fori_loop(0, D // TILE, query_tile, 0)

        def each(blocks, fresh):
            def step(kv_at, carry):
                attend(kv_at, m, blocks, fresh)
                return carry

            lax.fori_loop(0, KV_HEADS, step, 0)

        each((0,), True)

        @pl.when(place == 1)
        def _():
            kv_copy(m, 0, 1, 0, 1).wait_recv()
            each((1,), False)

        @pl.when(place == 2)
        def _():
            kv_copy(m, 0, 2, 0, 2).wait_recv()
            each((2,), False)
            kv_copy(m, 0, 1, 0, 2).wait_recv()
            each((1,), False)

        @pl.when(place == 3)
        def _():
            kv_copy(m, 0, 2, 0, 3).wait_recv()
            kv_copy(m, 2, 1, 0, 2).start()
            kv_copy(m, 0, 1, 0, 3).wait_recv()
            each((1, 2), False)

        def finish(kv_at, carry):
            one = pl.ds(kv_at, 1)
            total = s_lse[one, :]
            for g in range(GROUP):
                rows = at((kv_at * GROUP + g) * HEAD, HEAD, 64)
                value = s_att[rows, :] / total[:, g * toks : (g + 1) * toks]
                s_att[rows, :] = value
                s_context[rows, :] = value.astype(LOW)
            s_lse[one, :] = s_top[one, :] + jnp.log(total)
            return carry

        lax.fori_loop(0, KV_HEADS, finish, 0)

        def out_tile(i, carry):
            rows = at(i * TILE, TILE)
            s_hidden[rows, :] = x_now[rows, :] + dot(
                v_joint[:, at(qkv + i * TILE, TILE)], s_context[...], 0, 0
            )
            return carry

        lax.fori_loop(0, D // TILE, out_tile, 0)
        hidden = s_hidden[...]
        s_second[...] = (hidden * column_scale(hidden) * gains[:, 1:2]).astype(LOW)

        @pl.when(m == 0)
        def _():
            loads[1].wait()

        def gate_tile(i, carry):
            rows, up_rows = at(i * WIDE, WIDE), at(FF + i * WIDE, WIDE)
            gate = dot(v_gate_up[:, rows], s_second[...], 0, 0)
            up = dot(v_gate_up[:, up_rows], s_second[...], 0, 0)
            s_gu[rows, :] = gate
            s_gu[up_rows, :] = up
            s_inner[rows, :] = (gate * jax.nn.sigmoid(gate) * up).astype(LOW)
            return carry

        lax.fori_loop(0, FF // WIDE, gate_tile, 0)

        @pl.when(m == 0)
        def _():
            loads[2].wait()

        def down_tile(i, carry):
            rows = at(i * TILE, TILE)
            value = s_hidden[rows, :] + dot(v_down[:, rows], s_inner[...], 0, 0)
            x_now[rows, :] = value
            x_in[m, rows, :] = value.astype(LOW)
            return carry

        lax.fori_loop(0, D // TILE, down_tile, 0)

        @pl.when(section == 0)
        def _():
            x_copy(m).start()

        for save in saves(m):
            save.start()

        @pl.when(section == 1)
        def _():
            s_result[...] = x_now[...].T
            result_save(m).start()

        return carry

    lax.fori_loop(0, micros, micro, 0)
    for save in saves(micros - 1):
        save.wait()

    @pl.when(section == 1)
    def _():
        result_save(micros - 1).wait()

    for m in range(2):
        @pl.when(section == 0)
        def _(m=m):
            x_copy(m).wait_send()

        for who, copy in kv_sends(m):
            @pl.when(place == who)
            def _(copy=copy):
                copy.wait_send()

        @pl.when(place == 3)
        def _(m=m):
            kv_copy(m, 2, 1, 0, 2).wait_send()


def backward_kernel(
    ends, gains, cosine, sine, seg_row, seg_col, w_joint, w_gate_up, w_down,
    i_x, i_q, i_kv, i_att, i_lse, i_hidden, i_gu,
    o_both, o_mixed, o_hidden, o_grad, o_gains, o_result,
    v_joint, v_gate_up, v_down, g_in, g_now, s_x, s_q, s_kv, s_att, s_lse, s_hid, s_gu,
    s_both, s_mixed, s_hidden, s_grad, s_sum, s_context, s_delta, s_dq, s_dkv, kv_out, kv_in,
    s_gains, s_result, bias,
    w_sem, load_sem, save_sem, kv_send, kv_recv, x_send, x_recv,
):
    section = lax.axis_index("section")
    place = lax.axis_index("ctx")
    micros, toks = ends.shape[0], ends.shape[1]
    qkv = D + 2 * KVW
    w_loads = [
        pltpu.make_async_copy(src, dst, w_sem.at[i])
        for i, (src, dst) in enumerate(
            ((w_joint, v_joint), (w_gate_up, v_gate_up), (w_down, v_down))
        )
    ]

    def loads(m):
        pairs = (
            (i_gu, s_gu), (i_hidden, s_hid), (i_att, s_att), (i_q, s_q), (i_kv, s_kv),
            (i_lse, s_lse), (i_x, s_x),
        )
        return [pltpu.make_async_copy(a.at[m], b, load_sem.at[i]) for i, (a, b) in enumerate(pairs)]

    w_loads[2].start()
    for load in loads(0):
        load.start()
    w_loads[1].start()
    w_loads[0].start()
    greet([{"ctx": (place + i) % 4} for i in (1, 2, 3)] + [{"section": 1 - section}])
    s_gains[...] = jnp.zeros_like(s_gains)

    def saves(m):
        lanes = at(m * toks, toks)
        pairs = (
            (s_both, o_both.at[:, lanes]), (s_mixed, o_mixed.at[:, lanes]),
            (s_hidden, o_hidden.at[:, lanes]), (s_grad, o_grad.at[:, lanes]),
        )
        return [pltpu.make_async_copy(a, b, save_sem.at[i]) for i, (a, b) in enumerate(pairs)]

    def result_save(m):
        return pltpu.make_async_copy(s_result, o_result.at[m], save_sem.at[4])

    def g_copy(m):
        return remote(g_in.at[m], g_in.at[m], x_send.at[m], x_recv.at[m], {"section": 0})

    def kv_copy(m, source, slot, lane, to):
        return remote(
            kv_out.at[m, source], kv_in.at[m, slot], kv_send.at[m, lane], kv_recv.at[m, slot],
            {"ctx": to},
        )

    def kv_sends(m):
        return (
            (1, kv_copy(m, 0, 0, 0, 0)),
            (2, kv_copy(m, 0, 0, 0, 3)),
            (2, kv_copy(m, 1, 1, 1, 0)),
            (3, kv_copy(m, 0, 0, 0, 2)),
            (3, kv_copy(m, 1, 0, 1, 1)),
        )

    def block_grads(d, m, fresh):
        def step(kv_at, carry):
            rows = at(kv_at * HEAD, HEAD, 64)
            value_rows = at(KVW + kv_at * HEAD, HEAD, 64)
            one = pl.ds(kv_at, 1)
            query, grad = s_q[rows, :], s_context[rows, :]
            key, value = s_kv[d, rows, :], s_kv[d, value_rows, :]
            mask = bias[d]
            scores = dot(key, query, 0, 0) + jnp.concatenate([mask] * GROUP, axis=1)
            probs = jnp.exp(scores - s_lse[one, :])
            grad_probs = dot(value, grad, 0, 0)
            grad_scores = (probs * (grad_probs - s_delta[one, :])).astype(LOW)
            s_dkv[rows, :] = dot(query, grad_scores, 1, 1)
            s_dkv[value_rows, :] = dot(grad, probs.astype(LOW), 1, 1)
            grad_query = dot(key, grad_scores, 1, 0)
            if fresh:
                s_dq[rows, :] = grad_query
            else:
                s_dq[rows, :] = s_dq[rows, :] + grad_query
            return carry

        lax.fori_loop(0, KV_HEADS, step, 0)

    def norm_back(grad, source, gain, row):
        scale = column_scale(source)
        unit = source * scale
        product = grad * unit
        fold = product[:, :128]
        for i in range(1, toks // 128):
            fold = fold + product[:, i * 128 : (i + 1) * 128]
        s_gains[row] = s_gains[row] + fold
        inner = grad * gain
        return scale * (inner - unit * jnp.mean(inner * unit, axis=0, keepdims=True))

    def micro(m, carry):
        @pl.when(m > 0)
        def _():
            for save in saves(m - 1):
                save.wait()

            @pl.when(section == 0)
            def _():
                result_save(m - 1).wait()

        fill_bias(bias, seg_row, seg_col, m, place, toks)

        @pl.when(section == 1)
        def _():
            s_grad[...] = ends[m].astype(F32).T.astype(LOW)

        @pl.when(section == 0)
        def _():
            g_copy(m).wait_recv()
            s_grad[...] = g_in[m]

        @pl.when(m == 0)
        def _():
            w_loads[2].wait()

        now = loads(m)
        now[0].wait()

        def inner_tile(i, carry):
            rows, up_rows = at(i * TILE, TILE), at(FF + i * TILE, TILE)
            grad_inner = dot(v_down[rows, :], s_grad[...], 1, 0)
            gate, up = s_gu[rows, :], s_gu[up_rows, :]
            sig = jax.nn.sigmoid(gate)
            s_both[rows, :] = (grad_inner * up * sig * (1.0 + gate * (1.0 - sig))).astype(LOW)
            s_both[up_rows, :] = (grad_inner * (gate * sig)).astype(LOW)
            return carry

        lax.fori_loop(0, FF // TILE, inner_tile, 0)

        @pl.when(m == 0)
        def _():
            w_loads[1].wait()

        @pl.when(m + 1 < micros)
        def _():
            loads(m + 1)[0].start()

        def second_tile(i, carry):
            rows = at(i * TILE, TILE)
            s_sum[rows, :] = dot(v_gate_up[rows, :], s_both[...], 1, 0)
            return carry

        lax.fori_loop(0, D // TILE, second_tile, 0)
        now[1].wait()
        g_now[...] = s_grad[...].astype(F32) + norm_back(s_sum[...], s_hid[...], gains[:, 1:2], 1)
        s_hidden[...] = g_now[...].astype(LOW)

        @pl.when(m == 0)
        def _():
            w_loads[0].wait()

        for i in (2, 3, 4, 5):
            now[i].wait()

        def context_tile(i, carry):
            block = dot(v_joint[at(i * TILE, TILE), qkv:], s_hidden[...], 1, 0).astype(LOW)
            for head in range(TILE // HEAD):
                kv_at = i * (TILE // HEAD // GROUP) + head // GROUP
                g = head % GROUP
                part = block[head * HEAD : (head + 1) * HEAD]
                s_context[at(kv_at * HEAD, HEAD, 64), g * toks : (g + 1) * toks] = part
                seen = s_att[at(i * TILE + head * HEAD, HEAD, 64), :]
                s_delta[pl.ds(kv_at, 1), g * toks : (g + 1) * toks] = jnp.sum(
                    part.astype(F32) * seen, axis=0, keepdims=True
                )
            return carry

        lax.fori_loop(0, D // TILE, context_tile, 0)
        sends = kv_sends(m)

        @pl.when(place == 0)
        def _():
            block_grads(0, m, True)

        @pl.when(place == 1)
        def _():
            block_grads(1, m, True)
            kv_out[m, 0] = s_dkv[...].astype(LOW)
            sends[0][1].start()
            block_grads(0, m, False)

        @pl.when(place == 2)
        def _():
            block_grads(1, m, True)
            kv_out[m, 0] = s_dkv[...].astype(LOW)
            sends[1][1].start()
            block_grads(2, m, False)
            kv_out[m, 1] = s_dkv[...].astype(LOW)
            sends[2][1].start()
            block_grads(0, m, False)

        @pl.when(place == 3)
        def _():
            block_grads(2, m, True)
            kv_copy(m, 0, 0, 0, 3).wait_recv()
            kv_out[m, 1] = (s_dkv[...] + kv_in[m, 0].astype(F32)).astype(LOW)
            sends[4][1].start()
            block_grads(1, m, False)
            kv_out[m, 0] = s_dkv[...].astype(LOW)
            sends[3][1].start()
            block_grads(0, m, False)

        cos, sin = cosine[...], sine[...]

        def rotated_back(front, back):
            return jnp.concatenate([front * cos + back * sin, back * cos - front * sin], axis=0)

        def query_back(kv_at, carry):
            for g in range(GROUP):
                lanes = slice(g * toks, (g + 1) * toks)
                front = s_dq[at(kv_at * HEAD, HALF, 32), lanes] * SCALE
                back = s_dq[at(kv_at * HEAD + HALF, HALF, 32), lanes] * SCALE
                rows = at((kv_at * GROUP + g) * HEAD, HEAD, 64)
                s_mixed[rows, :] = rotated_back(front, back).astype(LOW)
            return carry

        lax.fori_loop(0, KV_HEADS, query_back, 0)

        def normed_tile(i, carry):
            rows = at(i * TILE, TILE)
            s_sum[rows, :] = dot(v_joint[rows, :D], s_mixed[:D, :], 1, 0)
            return carry

        lax.fori_loop(0, D // TILE, normed_tile, 0)

        @pl.when(place == 0)
        def _():
            kv_copy(m, 0, 0, 0, 0).wait_recv()
            kv_copy(m, 0, 1, 0, 0).wait_recv()
            s_dkv[...] = s_dkv[...] + kv_in[m, 0].astype(F32) + kv_in[m, 1].astype(F32)

        @pl.when((place == 1) | (place == 2))
        def _():
            kv_copy(m, 0, 0, 0, 0).wait_recv()
            s_dkv[...] = s_dkv[...] + kv_in[m, 0].astype(F32)

        for head in range(KV_HEADS):
            front = s_dkv[head * HEAD : head * HEAD + HALF, :]
            back = s_dkv[head * HEAD + HALF : (head + 1) * HEAD, :]
            s_mixed[D + head * HEAD : D + (head + 1) * HEAD, :] = rotated_back(front, back).astype(LOW)
        s_mixed[D + KVW : qkv, :] = s_dkv[KVW : 2 * KVW, :].astype(LOW)

        def rest_tile(i, carry):
            rows = at(i * TILE, TILE)
            s_sum[rows, :] = s_sum[rows, :] + dot(v_joint[rows, D:qkv], s_mixed[D:qkv, :], 1, 0)
            return carry

        lax.fori_loop(0, D // TILE, rest_tile, 0)
        now[6].wait()
        g_now[...] = g_now[...] + norm_back(s_sum[...], s_x[...].astype(F32), gains[:, 0:1], 0)

        @pl.when(section == 1)
        def _():
            g_in[m] = g_now[...].astype(LOW)
            g_copy(m).start()

        @pl.when(m + 1 < micros)
        def _():
            for load in loads(m + 1)[1:]:
                load.start()

        for save in saves(m):
            save.start()

        @pl.when(section == 0)
        def _():
            s_result[...] = g_now[...].T
            result_save(m).start()

        return carry

    lax.fori_loop(0, micros, micro, 0)
    gains_save = pltpu.make_async_copy(s_gains, o_gains, save_sem.at[5])
    gains_save.start()
    for save in saves(micros - 1):
        save.wait()

    @pl.when(section == 0)
    def _():
        result_save(micros - 1).wait()

    gains_save.wait()
    for m in range(2):
        @pl.when(section == 1)
        def _(m=m):
            g_copy(m).wait_send()

        for who, copy in kv_sends(m):
            @pl.when(place == who)
            def _(copy=copy):
                copy.wait_send()


def run_forward(ends, gains, cosine, sine, seg_row, seg_col, joint, gate_up, down):
    micros, toks = ends.shape[0], ends.shape[1]
    width = GROUP * toks
    vm, hbm = pl.BlockSpec(memory_space=pltpu.VMEM), pl.BlockSpec(memory_space=pl.ANY)
    sem = pltpu.SemaphoreType.DMA
    outs = [
        ((D, micros * toks), LOW), ((D, micros * toks), LOW), ((D, micros * toks), LOW),
        ((FF, micros * toks), LOW), ((micros, D, toks), LOW), ((micros, KVW, width), LOW),
        ((micros, 3, 2 * KVW, toks), LOW), ((micros, D, toks), F32), ((micros, 8, width), F32),
        ((micros, D, toks), F32), ((micros, 2 * FF, toks), F32), ((micros, toks, D), F32),
    ]
    scratch = [
        (joint.shape, LOW), (gate_up.shape, LOW), (down.shape, LOW),
        ((micros, D, toks), LOW), ((D, toks), F32),
        ((D, toks), LOW), ((D, toks), LOW), ((D, toks), LOW), ((FF, toks), LOW), ((D, toks), LOW),
        ((KVW, width), LOW), ((micros, 3, 2 * KVW, toks), LOW), ((D, toks), F32), ((8, width), F32),
        ((8, width), F32), ((D, toks), F32), ((2 * FF, toks), F32), ((toks, D), F32), ((3, toks, toks), F32),
    ]
    return pl.pallas_call(
        forward_kernel,
        out_shape=tuple(jax.ShapeDtypeStruct(s, t) for s, t in outs),
        in_specs=[vm] * 6 + [hbm] * 3,
        out_specs=(hbm,) * len(outs),
        scratch_shapes=[pltpu.VMEM(s, t) for s, t in scratch]
        + [sem((3,)), sem((12,)), sem((micros, 2)), sem((micros, 3)), sem((micros,)), sem((micros,))],
        compiler_params=pltpu.CompilerParams(
            collective_id=3, has_side_effects=True, vmem_limit_bytes=62 * 2**20
        ),
        name="layer_forward",
    )(ends, gains, cosine, sine, seg_row, seg_col, joint, gate_up, down)


def run_backward(ends, gains, cosine, sine, seg_row, seg_col, joint, gate_up, down, saved):
    micros, toks = ends.shape[0], ends.shape[1]
    width = GROUP * toks
    vm, hbm = pl.BlockSpec(memory_space=pltpu.VMEM), pl.BlockSpec(memory_space=pl.ANY)
    sem = pltpu.SemaphoreType.DMA
    qkv = D + 2 * KVW
    outs = [
        ((2 * FF, micros * toks), LOW), ((qkv, micros * toks), LOW), ((D, micros * toks), LOW),
        ((D, micros * toks), LOW), ((2, D, 128), F32), ((micros, toks, D), F32),
    ]
    scratch = [
        (joint.shape, LOW), (gate_up.shape, LOW), (down.shape, LOW),
        ((micros, D, toks), LOW), ((D, toks), F32),
        ((D, toks), LOW), ((KVW, width), LOW), ((3, 2 * KVW, toks), LOW), ((D, toks), F32), ((8, width), F32),
        ((D, toks), F32), ((2 * FF, toks), F32),
        ((2 * FF, toks), LOW), ((qkv, toks), LOW), ((D, toks), LOW), ((D, toks), LOW), ((D, toks), F32),
        ((KVW, width), LOW), ((8, width), F32), ((KVW, width), F32), ((2 * KVW, toks), F32),
        ((micros, 2, 2 * KVW, toks), LOW), ((micros, 2, 2 * KVW, toks), LOW),
        ((2, D, 128), F32), ((toks, D), F32), ((3, toks, toks), F32),
    ]
    return pl.pallas_call(
        backward_kernel,
        out_shape=tuple(jax.ShapeDtypeStruct(s, t) for s, t in outs),
        in_specs=[vm] * 6 + [hbm] * 10,
        out_specs=(hbm,) * len(outs),
        scratch_shapes=[pltpu.VMEM(s, t) for s, t in scratch]
        + [sem((3,)), sem((7,)), sem((6,)), sem((micros, 2)), sem((micros, 2)), sem((micros,)), sem((micros,))],
        compiler_params=pltpu.CompilerParams(
            collective_id=4, has_side_effects=True, vmem_limit_bytes=62 * 2**20
        ),
        name="layer_backward",
    )(ends, gains, cosine, sine, seg_row, seg_col, joint, gate_up, down, *saved)


def small_mesh():
    return lax.axis_size("ctx") == 4 and lax.axis_size("fsdp") == 4


def whole_weights(w_qkv, w_out, w_gate_up, w_down):
    return tuple(
        lax.all_gather(w, "fsdp", axis=0, tiled=True) for w in (w_qkv, w_out, w_gate_up, w_down)
    )


def owned_grads(lefts, rights):
    return tuple(
        lax.psum_scatter(
            outer_product(left, right).astype(jnp.bfloat16),
            ("ctx", "fsdp"),
            scatter_dimension=0,
            tiled=True,
        ).astype(jnp.float32)
        for left, right in zip(lefts, rights)
    )


def local_small(ends, segment_ids, w_qkv, w_out, w_gate_up, w_down, gains):
    section_index = lax.axis_index("section")
    tok_rows = ends.shape[3]
    local_ends = ends[0, :, 0]
    seg_local = segment_ids[:, 0]
    seg_whole = lax.all_gather(seg_local, "ctx", axis=1, tiled=True)
    query_pos = lax.axis_index("ctx") * tok_rows + jnp.arange(tok_rows, dtype=jnp.int32)
    frequency = 10000.0 ** (-(jnp.arange(HEAD // 2).astype(jnp.float32) * 2.0 / HEAD))
    angle_table = frequency[:, None] * query_pos.astype(jnp.float32)[None, :]
    shared = (
        local_ends,
        gains[0].T,
        jnp.cos(angle_table),
        jnp.sin(angle_table),
        seg_local[:, None, :],
        seg_whole[:, :, None],
    ) + tuple(gather_weights(jnp.concatenate([w_qkv[0], w_out[0]], axis=1), w_gate_up[0], w_down[0]))
    normed, context, second, inner, *saved, result = run_forward(*shared)
    x, q, kv, att, lse, hidden, gate_up = saved
    both, mixed, hidden_low, grad, gain_parts, input_grads = run_backward(
        *shared, (x, q, kv, att, lse, hidden, gate_up)
    )
    gain_rows = jnp.sum(gain_parts, axis=-1).reshape(2, 16, D // 16)
    gain_tiles = jnp.pad(jnp.swapaxes(gain_rows, 0, 1), ((0, 0), (0, 6), (0, 128 - D // 16)))
    g_down, g_gate_up, g_qkv, g_out, gain = reduce_grads(
        (normed, context, second, inner), (both, mixed, hidden_low, grad), gain_tiles
    )
    ends_out = jnp.where(section_index == 0, input_grads, result)[None, :, None]
    return (
        ends_out, g_qkv[None], g_out[None], g_gate_up[None], g_down[None],
        gain[None, :2, : D // 16],
    )


def local(ends, segment_ids, w_qkv, w_out, w_gate_up, w_down, gains):
    if small_mesh():
        return local_small(ends, segment_ids, w_qkv, w_out, w_gate_up, w_down, gains)
    section_index = lax.axis_index("section")
    micro_count = ends.shape[1]
    tok_rows = ends.shape[3]
    local_ends = ends[0, :, 0]
    seg_local = segment_ids[:, 0]
    seg_whole = lax.all_gather(seg_local, "ctx", axis=1, tiled=True)
    query_pos = lax.axis_index("ctx") * tok_rows + jnp.arange(tok_rows, dtype=jnp.int32)
    frequency = 10000.0 ** (-(jnp.arange(HEAD // 2).astype(jnp.float32) * 2.0 / HEAD))
    angle_table = query_pos.astype(jnp.float32)[:, None] * frequency[None, :]
    cosine = jnp.cos(angle_table)[:, None, :]
    sine_table = jnp.sin(angle_table)[:, None, :]
    gain_pair = gains[0]
    weights = whole_weights(w_qkv[0], w_out[0], w_gate_up[0], w_down[0])
    arrived = jnp.zeros((tok_rows, D), jnp.bfloat16)
    store_bufs = None
    outputs = jnp.zeros((micro_count + 1, tok_rows, D), jnp.float32)
    for tick_num in range(micro_count + 1):
        batch_index = tick_num - section_index
        is_valid = (batch_index >= 0) & (batch_index < micro_count)
        clipped = jnp.clip(batch_index, 0, micro_count - 1)
        slot_index = jnp.where(is_valid, batch_index, micro_count)
        own_rows = lax.dynamic_index_in_dim(local_ends, clipped, 0, keepdims=False)
        layer_in = jnp.where(section_index == 0, own_rows, arrived)
        seg_rows = lax.dynamic_index_in_dim(seg_local, clipped, 0, keepdims=False)
        seg_full = lax.dynamic_index_in_dim(seg_whole, clipped, 0, keepdims=False)
        result, saved_acts = layer_forward(
            layer_in.astype(jnp.float32),
            weights,
            gain_pair,
            seg_rows,
            seg_full,
            query_pos,
            cosine,
            sine_table,
        )
        if tick_num == 0:
            store_bufs = jax.tree.map(
                lambda update: jnp.zeros((micro_count + 1,) + update.shape, update.dtype),
                saved_acts,
            )
        store_bufs = jax.tree.map(
            lambda buffer, update: lax.dynamic_update_index_in_dim(buffer, update, slot_index, 0),
            store_bufs,
            saved_acts,
        )
        outputs = lax.dynamic_update_index_in_dim(outputs, result, slot_index, 0)
        arrived = shifted(result.astype(jnp.bfloat16), "section", 1)
    operand_bufs = None
    gain_sums = jnp.zeros((2, D), jnp.float32)
    arrived_grad = jnp.zeros((tok_rows, D), jnp.bfloat16)
    input_grads = jnp.zeros((micro_count + 1, tok_rows, D), jnp.float32)
    for tick_num in range(micro_count + 1):
        batch_index = tick_num - (1 - section_index)
        is_valid = (batch_index >= 0) & (batch_index < micro_count)
        clipped = jnp.clip(batch_index, 0, micro_count - 1)
        slot_index = jnp.where(is_valid, batch_index, micro_count)
        own_rows = lax.dynamic_index_in_dim(local_ends, clipped, 0, keepdims=False)
        incoming = jnp.where(section_index == 1, own_rows, arrived_grad)
        incoming = jnp.where(is_valid, incoming, jnp.zeros_like(incoming))
        seg_rows = lax.dynamic_index_in_dim(seg_local, clipped, 0, keepdims=False)
        seg_full = lax.dynamic_index_in_dim(seg_whole, clipped, 0, keepdims=False)
        saved_acts = jax.tree.map(
            lambda buffer: lax.dynamic_index_in_dim(buffer, clipped, 0, keepdims=False), store_bufs
        )
        grad_input, operand_pairs, gain_terms = layer_backward(
            incoming,
            saved_acts,
            weights,
            gain_pair,
            seg_rows,
            seg_full,
            query_pos,
            cosine,
            sine_table,
        )
        if tick_num == 0:
            operand_bufs = jax.tree.map(
                lambda update: jnp.zeros((micro_count + 1,) + update.shape, update.dtype),
                operand_pairs,
            )
        operand_bufs = jax.tree.map(
            lambda buffer, update: lax.dynamic_update_index_in_dim(buffer, update, slot_index, 0),
            operand_bufs,
            operand_pairs,
        )
        gain_sums = gain_sums + gain_terms
        input_grads = lax.dynamic_update_index_in_dim(input_grads, grad_input, slot_index, 0)
        arrived_grad = shifted(grad_input.astype(jnp.bfloat16), "section", -1)
    operands = [buffer[:micro_count].reshape(-1, buffer.shape[-1]) for buffer in operand_bufs]
    g_qkv, g_out, g_gate_up, g_down = owned_grads(operands[:4], operands[4:])
    g_gains = lax.psum_scatter(gain_sums, ("ctx", "fsdp"), scatter_dimension=1, tiled=True)
    final_rows = jnp.where(section_index == 0, input_grads[:micro_count], outputs[:micro_count])
    ends_out = final_rows[None, :, None]
    return (ends_out, g_qkv[None], g_out[None], g_gate_up[None], g_down[None], g_gains[None])


def solution(mesh):
    in_specs = (
        P("section", None, "fsdp", "ctx", None),
        P(None, "fsdp", "ctx"),
        P("section", "fsdp", None),
        P("section", "fsdp", None),
        P("section", "fsdp", None),
        P("section", "fsdp", None),
        P("section", None, None),
    )
    out_specs = (
        P("section", None, "fsdp", "ctx", None),
        P("section", ("ctx", "fsdp"), None),
        P("section", ("ctx", "fsdp"), None),
        P("section", ("ctx", "fsdp"), None),
        P("section", ("ctx", "fsdp"), None),
        P("section", None, ("ctx", "fsdp")),
    )
    return jax.shard_map(local, mesh=mesh, in_specs=in_specs, out_specs=out_specs, check_vma=False)
```

profile of v0, /device:TPU:0, one launch (start us, length us, event | category | flops | bytes accessed | tf_op | source)
XLA Modules:
  0.0 548.7 jit_solution(6707852529749418969)
XLA Ops:
  0.6 0.0 copy-start.2
  0.7 6.4 %all-gather = s32[2,1,1024]{2,1,0:T(1,128)S(1)} all-gather(s32[2,1,256]{2,1,0:T(1,128)} %seg_row.3), channel_id=2, replica_groups=mesh['section'=2,'ctx'=4,'fsdp'=4] {'ctx'}, dimensions={2}, use_global_device_ids=true | all-gather | bytes 10240 | tf_op jit(solution)/shard_map/all_gather | solution.py:1507
  7.1 0.8 multiply_sine_fusion
  8.0 1.8 copy.16
  9.7 1.3 broadcast_in_dim.30.seg_col
  11.0 0.0 copy-done.2
  11.0 2.5 pad_maximum_fusion.qo
  13.5 134.5 %weights_gather.1 = (bf16[1152,3072]{1,0:T(8,128)(2,1)}, bf16[1152,6144]{1,0:T(8,128)(2,1)}, bf16[3072,1152]{1,0:T(8,128)(2,1)}) custom-call(bf16[288,3072]{1,0:T(8,128)(2,1)} %pad_maximum_fusion.qo, bf16[288,6144]{1,0:T(8,128)(2,1)} %bitcast.25, bf16[768,1152]{1,0:T(8,128)(2,1)} %bitcast.26), custom_call_target="tpu_custom_call" | custom-call | tf_op jit(solution)/shard_map/weights_gather/pallas_call | solution.py:466
  148.1 49.7 %layer_forward.1 = (bf16[1152,512]{1,0:T(8,128)(2,1)}, bf16[1152,512]{1,0:T(8,128)(2,1)}, bf16[1152,512]{1,0:T(8,128)(2,1)}, bf16[3072,512]{1,0:T(8,128)(2,1)}, ...) custom-call(bf16[2,256,1152]{2,1,0:T(8,128)(2,1)} %bitcast.23, ...), custom_call_target="tpu_custom_call" | custom-call | tf_op jit(solution)/shard_map/layer_forward/pallas_call | solution.py:1432
  197.7 164.3 %layer_backward.1 = (bf16[6144,512]{1,0:T(8,128)(2,1)}, bf16[1920,512]{1,0:T(8,128)(2,1)}, bf16[1152,512]{1,0:T(8,128)(2,1)}, bf16[1152,512]{1,0:T(8,128)(2,1)},...) custom-call(bf16[2,256,1152]{2,1,0:T(8,128)(2,1)} %bitcast.24, f32[1152,2]{1,0:T(8,128)} %bitcast.22, ...), custom_call_target="tpu_custom_call" | custom-call | tf_op jit(solution)/shard_map/layer_backward/pallas_call | solution.py:1466
  362.1 0.0 copy-start.1
  362.1 3.4 select_bitcast_fusion
  365.5 0.0 copy-done.1
  365.5 0.4 reduce_sum.9
  365.9 0.1 reshape.27
  366.0 0.6 pad.4.gain_tiles
  366.6 174.9 %grads_reduce.1 = (f32[192,1152]{1,0:T(8,128)}, f32[72,6144]{1,0:T(8,128)}, f32[72,1920]{1,0:T(8,128)}, f32[72,1152]{1,0:T(8,128)}, f32[8,128]{1,0:T(8,128)}) custom-call(bf16[3072,512]{1,0:T(8,128)(2,1)} %get-tuple-element.44.inner_h, bf16[1152,512]{1,0:T(8,128)(2,1)} %get-tuple-element.45.grad_h, bf16[1152,512]{1,0:T(8,128)(2,1)} %get-tuple-element.46.second_h, ...), custom_call_target="tpu_custom_call" | custom-call | tf_op jit(solution)/shard_map/grads_reduce/pallas_call | solution.py:787
  541.5 0.0 copy-start
  541.5 1.4 slice_bitcast_fusion
  542.9 1.9 copy.27
  544.8 0.0 copy-start.3
  544.8 1.8 copy.28
  546.6 0.0 copy-done
  546.6 1.2 copy.29
  547.8 0.0 copy-done.3
  547.8 0.9 copy.30
  (4 shorter events, 0.1 us)
Async XLA Ops:
  0.6 10.4 %copy-start.2 = (bf16[1,288,1920]{2,1,0:T(8,128)(2,1)S(1)}, bf16[1,288,1920]{2,1,0:T(8,128)(2,1)}, u32[]{:S(2)}) copy-start(bf16[1,288,1920]{2,1,0:T(8,128)(2,1)} %param.9) | copy-start | bytes 3317764
  362.1 3.4 copy-start.1
  541.5 5.1 copy-start
  544.8 3.0 copy-start.3
where the time goes:
time: 549 us
  Pallas kernels  523 us (95%)
  local copies, waits for them, and re-layouts  11 us (2%)
  other arithmetic  7.16 us (1%)
  blocking collectives  6.43 us (1%)
    pallas_call x1, Pallas kernels, reduce_grads(): pl.pallas_call(reduce_kernel, out_shape=tuple((jax.ShapeDtypeStruct(s, f3...  175 us
    pallas_call x1, Pallas kernels, run_backward(): pl.pallas_call(backward_kernel, out_shape=tuple((jax.ShapeDtypeStruct(s,...  164 us
    pallas_call x1, Pallas kernels, gather_weights(): pl.pallas_call(gather_kernel, out_shape=tuple((jax.ShapeDtypeStruct((size...  135 us
    pallas_call x1, Pallas kernels, run_forward(): pl.pallas_call(forward_kernel, out_shape=tuple((jax.ShapeDtypeStruct(s, t...  49.7 us

commit v1 on v0

--- a/solution.py
+++ b/solution.py
@@ -327,154 +327,6 @@
     return (grad_input, operand_pairs, jnp.stack([gain_one, gain_two]))
 
 
-def gather_kernel(qo, gu, dn, fqo, fgu, fdn, own_sem, back_sem, zs, zr, ys, yr, cs, cr, es, er):
-    place = lax.axis_index("ctx")
-    z = lax.axis_index("fsdp")
-    last = lax.axis_size("fsdp") - 1
-    y, k = place // 2, place % 2
-    y_mate = {"ctx": (1 - y) * 2 + k}
-    k_mate = {"ctx": y * 2 + 1 - k}
-    width = qo.shape[0]
-    deep = dn.shape[0]
-    half = width // 2
-    chunks = [(0, p) for p in range(3)] + [(1, p) for p in range(3)] + [(2, p) for p in range(2)]
-    wholes = (fqo, fgu, fdn)
-    owns = (qo, gu, dn)
-
-    def view(refs, shard, yy, kk, chunk):
-        m, p = chunk
-        ref = refs[m]
-        if m == 2:
-            rows = deep // 8
-            first = shard * deep + (yy * 2 + kk) * (deep // 4) + p * rows
-            return ref.at[pl.ds(pl.multiple_of(first, 16), rows), :]
-        rows = half // 3
-        cols = ref.shape[1] // 2
-        first = shard * width + yy * half + p * rows
-        return ref.at[pl.ds(pl.multiple_of(first, 16), rows), pl.ds(pl.multiple_of(kk * cols, 128), cols)]
-
-    barrier = pltpu.get_barrier_semaphore()
-    for mate in (y_mate, k_mate):
-        pl.semaphore_signal(barrier, inc=1, device_id=mate, device_id_type=MESH)
-
-    @pl.when(z > 0)
-    def _():
-        pl.semaphore_signal(barrier, inc=1, device_id={"fsdp": z - 1}, device_id_type=MESH)
-
-    @pl.when(z < last)
-    def _():
-        pl.semaphore_signal(barrier, inc=1, device_id={"fsdp": z + 1}, device_id_type=MESH)
-
-    pl.semaphore_wait(barrier, 2 + jnp.where(z > 0, 1, 0) + jnp.where(z < last, 1, 0))
-
-    def z_copy(shard, j, to, first, back):
-        chunk = chunks[j]
-        src = view(owns, 0, y, k, chunk) if first else view(wholes, shard, y, k, chunk)
-        return pltpu.make_async_remote_copy(
-            src_ref=src, dst_ref=view(wholes, shard, y, k, chunk),
-            send_sem=back_sem.at[j] if back else zs.at[shard, j], recv_sem=zr.at[shard, j],
-            device_id={"fsdp": to}, device_id_type=MESH)
-
-    def mate_copy(shard, j, yy, mate, send, recv):
-        chunk = chunks[j]
-        ref = view(wholes, shard, yy, k, chunk)
-        return pltpu.make_async_remote_copy(
-            src_ref=ref, dst_ref=ref, send_sem=send.at[shard, j], recv_sem=recv.at[shard, j],
-            device_id=mate, device_id_type=MESH)
-
-    def arrive(shard, j, yy, kk, recv):
-        ref = view(wholes, shard, yy, kk, chunks[j])
-        pltpu.make_async_remote_copy(
-            src_ref=ref, dst_ref=ref, send_sem=recv.at[shard, j], recv_sem=recv.at[shard, j],
-            device_id=k_mate, device_id_type=MESH).wait_recv()
-
-    for j in range(len(chunks)):
-        @pl.when(z < last)
-        def _():
-            z_copy(z, j, z + 1, True, False).start()
-
-        @pl.when(z > 0)
-        def _():
-            z_copy(z, j, z - 1, True, True).start()
-    locals_ = []
-    for m in range(3):
-        rows = owns[m].shape[0]
-        locals_.append(pltpu.make_async_remote_copy(
-            src_ref=owns[m], dst_ref=wholes[m].at[pl.ds(pl.multiple_of(z * rows, 16), rows), :],
-            send_sem=own_sem.at[0, m], recv_sem=own_sem.at[1, m], device_id=k_mate, device_id_type=MESH))
-    for copy in locals_:
-        copy.start()
-
-    def sides(d):
-        return ((z - d >= 0, z - d, z + 1, z < last), (z + d <= last, z + d, z - 1, z > 0))
-
-    def relay(d, j):
-        for valid, shard, onward, more in sides(d):
-            @pl.when(valid)
-            def _():
-                arrive(shard, j, y, k, zr)
-                if d < 3:
-                    @pl.when(more)
-                    def _():
-                        z_copy(shard, j, onward, False, False).start()
-                mate_copy(shard, j, y, y_mate, ys, yr).start()
-                mate_copy(shard, j, y, k_mate, cs, cr).start()
-
-    def across(d, j):
-        for valid, shard, onward, more in sides(d):
-            @pl.when(valid)
-            def _():
-                arrive(shard, j, 1 - y, k, yr)
-                mate_copy(shard, j, 1 - y, k_mate, es, er).start()
-
-    order = [(d, j) for d in (1, 2, 3) for j in range(len(chunks))]
-    lag = 1
-    for i, (d, j) in enumerate(order):
-        relay(d, j)
-        if i >= lag:
-            across(*order[i - lag])
-    for d, j in order[len(order) - lag:]:
-        across(d, j)
-    for d, j in order:
-        for valid, shard, onward, more in sides(d):
-            @pl.when(valid)
-            def _():
-                arrive(shard, j, y, 1 - k, cr)
-                arrive(shard, j, 1 - y, 1 - k, er)
-                mate_copy(shard, j, y, y_mate, ys, yr).wait_send()
-                mate_copy(shard, j, y, k_mate, cs, cr).wait_send()
-                mate_copy(shard, j, 1 - y, k_mate, es, er).wait_send()
-                if d < 3:
-                    @pl.when(more)
-                    def _():
-                        z_copy(shard, j, onward, False, False).wait_send()
-    for j in range(len(chunks)):
-        @pl.when(z < last)
-        def _():
-            z_copy(z, j, z + 1, True, False).wait_send()
-
-        @pl.when(z > 0)
-        def _():
-            z_copy(z, j, z - 1, True, True).wait_send()
-    for copy in locals_:
-        copy.wait()
-
-
-def gather_weights(qo, gu, dn):
-    size = lax.axis_size("fsdp")
-    any_spec = pl.BlockSpec(memory_space=pl.ANY)
-    return pl.pallas_call(
-        gather_kernel,
-        out_shape=tuple(jax.ShapeDtypeStruct((size * w.shape[0], w.shape[1]), w.dtype) for w in (qo, gu, dn)),
-        in_specs=[any_spec] * 3,
-        out_specs=(any_spec,) * 3,
-        scratch_shapes=[pltpu.SemaphoreType.DMA((2, 3)), pltpu.SemaphoreType.DMA((8,))]
-        + [pltpu.SemaphoreType.DMA((4, 8))] * 8,
-        compiler_params=pltpu.CompilerParams(collective_id=1, has_side_effects=True),
-        name="weights_gather",
-    )(qo, gu, dn)
-
-
 DOWN_COLS = 128
 WIDE_COLS = 384
 NEAR, MID, FAR, SUMS = 2, 4, 8, 12
@@ -831,62 +683,248 @@
     )
 
 
-def fill_bias(bias, seg_row, seg_col, m, place, toks):
-    own = seg_row[m]
+def fill_bias(bias, segments, m, place, toks):
+    own = segments[place, pl.ds(m, 1), :]
     rows = lax.broadcasted_iota(jnp.int32, (toks, toks), 0)
     cols = lax.broadcasted_iota(jnp.int32, (toks, toks), 1)
     for d in range(3):
-        first = jnp.maximum(place - d, 0) * toks
-        keys = seg_col[m, pl.ds(pl.multiple_of(first, 128), toks), :]
+        seen = segments[jnp.maximum(place - d, 0), pl.ds(m, 1), :]
+        keys = jnp.broadcast_to(seen, (8, toks)).T[:, 0:1]
         allowed = keys == own
         if d == 0:
             allowed = allowed & (rows <= cols)
         bias[d] = jnp.where(allowed, 0.0, NONE)
 
 
+def gain_columns(gains, columns):
+    for row in range(2):
+        columns[:, row : row + 1] = jnp.broadcast_to(gains[row : row + 1, :], (8, D)).T[:, 0:1]
+
+
+JOINT_CHUNKS, WIDE_CHUNKS, DOWN_CHUNKS = 3, 3, 4
+CHUNKS = JOINT_CHUNKS + WIDE_CHUNKS + DOWN_CHUNKS
+SLAB = 1024
+
+
 def forward_kernel(
-    ends, gains, cosine, sine, seg_row, seg_col, w_joint, w_gate_up, w_down,
+    ends, gains, cosine, sine, seg_own, w_qkv, w_out, w_gate_up, w_down,
+    f_joint, f_gate_up, f_down, o_seg,
     o_normed, o_context, o_second, o_inner, o_x, o_q, o_kv, o_att, o_lse, o_hidden, o_gu, o_result,
-    v_joint, v_gate_up, v_down, x_in, x_now, s_normed, s_context, s_second, s_inner, s_x,
-    s_q, s_kv, s_att, s_top, s_lse, s_hidden, s_gu, s_result, bias,
-    w_sem, save_sem, kv_send, kv_recv, x_send, x_recv,
+    t_joint, t_gate_up, t_down, stage, stage_down, x_in, x_now, s_normed, s_context, s_second,
+    s_inner, s_x, s_q, s_kv, s_att, s_top, s_lse, s_hidden, s_gu, s_result, bias, segments, columns,
+    stage_sem, seg_sem, save_sem, kv_send, kv_recv, x_send, x_recv,
+    own_sem, back_sem, zs, zr, ys, yr, cs, cr, es, er,
 ):
     section = lax.axis_index("section")
     place = lax.axis_index("ctx")
+    z = lax.axis_index("fsdp")
+    last = lax.axis_size("fsdp") - 1
+    y, k = place // 2, place % 2
+    y_mate = {"ctx": (1 - y) * 2 + k}
+    k_mate = {"ctx": y * 2 + 1 - k}
     micros, toks = ends.shape[0], ends.shape[1]
     qkv = D + 2 * KVW
-    loads = [
-        pltpu.make_async_copy(src, dst, w_sem.at[i])
-        for i, (src, dst) in enumerate(
-            ((w_joint, v_joint), (w_gate_up, v_gate_up), (w_down, v_down))
+    width, deep = w_gate_up.shape[0], w_down.shape[0]
+    half, joint_half, wide_half = width // 2, f_joint.shape[1] // 2, f_gate_up.shape[1] // 2
+
+    barrier = pltpu.get_barrier_semaphore()
+    for peer in [{"ctx": (place + i) % 4} for i in (1, 2, 3)] + [{"section": 1 - section}]:
+        pl.semaphore_signal(barrier, inc=1, device_id=peer, device_id_type=MESH)
+
+    @pl.when(z > 0)
+    def _():
+        pl.semaphore_signal(barrier, inc=1, device_id={"fsdp": z - 1}, device_id_type=MESH)
+
+    @pl.when(z < last)
+    def _():
+        pl.semaphore_signal(barrier, inc=1, device_id={"fsdp": z + 1}, device_id_type=MESH)
+
+    pl.semaphore_wait(barrier, 4 + jnp.where(z > 0, 1, 0) + jnp.where(z < last, 1, 0))
+
+    def view(shard, yy, kk, j, own=False):
+        if j < JOINT_CHUNKS:
+            rows = half // JOINT_CHUNKS
+            return f_joint.at[
+                at(shard * width + yy * half + j * rows, rows, 16), at(kk * joint_half, joint_half)
+            ]
+        j = j - JOINT_CHUNKS
+        if j < WIDE_CHUNKS:
+            cols = wide_half // WIDE_CHUNKS
+            ref, first = (w_gate_up, 0) if own else (f_gate_up, shard * width)
+            return ref.at[at(first + yy * half, half, 16), at(kk * wide_half + j * cols, cols)]
+        j = j - WIDE_CHUNKS
+        rows = deep // 4 // DOWN_CHUNKS
+        ref, first = (w_down, 0) if own else (f_down, shard * deep)
+        return ref.at[at(first + (yy * 2 + kk) * (deep // 4) + j * rows, rows, 16), :]
+
+    def z_copy(shard, j, to, own, back):
+        ref = view(shard, y, k, j)
+        src = view(shard, y, k, j, True) if own and j >= JOINT_CHUNKS else ref
+        return remote(
+            src, ref, back_sem.at[j] if back else zs.at[shard, j], zr.at[shard, j], {"fsdp": to}
         )
+
+    def own_start(j, to, back):
+        if j >= JOINT_CHUNKS:
+            z_copy(z, j, to, True, back).start()
+            return
+        rows = half // JOINT_CHUNKS
+        here = at(y * half + j * rows, rows, 16)
+        there = at(z * width + y * half + j * rows, rows, 16)
+        send, recv = back_sem.at[j] if back else zs.at[z, j], zr.at[z, j]
+
+        @pl.when(k == 0)
+        def _():
+            remote(
+                w_qkv.at[here, 0:joint_half], f_joint.at[there, 0:joint_half], send, recv, {"fsdp": to}
+            ).start()
+
+        @pl.when(k == 1)
+        def _():
+            remote(
+                w_qkv.at[here, joint_half:qkv], f_joint.at[there, joint_half:qkv], send, recv, {"fsdp": to}
+            ).start()
+            remote(w_out.at[here, :], f_joint.at[there, qkv:], send, recv, {"fsdp": to}).start()
+
+    def own_sends(j):
+        @pl.when(z < last)
+        def _():
+            own_start(j, z + 1, False)
+
+        @pl.when(z > 0)
+        def _():
+            own_start(j, z - 1, True)
+
+    def mate_copy(shard, j, yy, mate, send, recv):
+        ref = view(shard, yy, k, j)
+        return remote(ref, ref, send.at[shard, j], recv.at[shard, j], mate)
+
+    def arrive(shard, j, yy, kk, recv):
+        ref = view(shard, yy, kk, j)
+        remote(ref, ref, recv.at[shard, j], recv.at[shard, j], k_mate).wait_recv()
+
+    rows_z, rows_deep = at(z * width, width, 16), at(z * deep, deep, 16)
+    own_pairs = (
+        (w_qkv, f_joint.at[rows_z, 0:qkv]), (w_out, f_joint.at[rows_z, qkv:]),
+        (w_gate_up, f_gate_up.at[rows_z, :]), (w_down, f_down.at[rows_deep, :]),
+    )
+    own_copies = [
+        remote(a, b, own_sem.at[0, i], own_sem.at[1, i], k_mate) for i, (a, b) in enumerate(own_pairs)
     ]
-    for load in loads:
-        load.start()
-    greet([{"ctx": (place + i) % 4} for i in (1, 2, 3)] + [{"section": 1 - section}])
+
+    def sides(d):
+        return ((z - d >= 0, z - d, z + 1, z < last), (z + d <= last, z + d, z - 1, z > 0))
+
+    def relay(d, j):
+        for valid, shard, onward, more in sides(d):
+            @pl.when(valid)
+            def _(shard=shard, onward=onward, more=more):
+                arrive(shard, j, y, k, zr)
+                if d < 3:
+                    @pl.when(more)
+                    def _():
+                        z_copy(shard, j, onward, False, False).start()
+                mate_copy(shard, j, y, y_mate, ys, yr).start()
+                mate_copy(shard, j, y, k_mate, cs, cr).start()
+
+    def across(d, j):
+        for valid, shard, onward, more in sides(d):
+            @pl.when(valid)
+            def _(shard=shard):
+                arrive(shard, j, 1 - y, k, yr)
+                mate_copy(shard, j, 1 - y, k_mate, es, er).start()
+
+    def complete(d, j):
+        for valid, shard, onward, more in sides(d):
+            @pl.when(valid)
+            def _(shard=shard):
+                arrive(shard, j, y, 1 - k, cr)
+                arrive(shard, j, 1 - y, 1 - k, er)
+
+    first_down = JOINT_CHUNKS + WIDE_CHUNKS
+    order = [(d, j) for d in (1, 2, 3) for j in range(JOINT_CHUNKS)]
+    order += [(d, j) for d in (1, 2, 3) for j in range(JOINT_CHUNKS, CHUNKS)]
+    refill = {2: (3,), 3: (4,), 4: (5,), 5: (6, 7), 6: (8, 9)}
+    done = {"relay": 0, "across": 0}
+
+    def pump(upto, lag=3):
+        while done["relay"] < min(upto, len(order)):
+            relay(*order[done["relay"]])
+            for extra in refill.get(done["relay"], ()):
+                own_sends(extra)
+            done["relay"] += 1
+            while done["across"] < done["relay"] - lag:
+                across(*order[done["across"]])
+                done["across"] += 1
+
+    def flush(upto):
+        while done["across"] < upto:
+            across(*order[done["across"]])
+            done["across"] += 1
+
+    def turn_slabs(ref, out, slabs, first, end):
+        rows = slice(first, end)
+        copies = [
+            pltpu.make_async_copy(
+                ref.at[rows, q * SLAB : (q + 1) * SLAB], stage.at[i, rows, :], stage_sem.at[i]
+            )
+            for i, q in enumerate(slabs)
+        ]
+        for copy in copies:
+            copy.start()
+        for i, q in enumerate(slabs):
+            copies[i].wait()
+
+            def step(c, carry, i=i, q=q):
+                cols = at(c * 256, 256)
+                out[at(q * SLAB + c * 256, 256), rows] = stage[i, rows, cols].T
+                return carry
+
+            lax.fori_loop(0, SLAB // 256, step, 0)
+
+    third = D // 3
+
+    def turn_near(ref, out, slabs):
+        for when, first, end in (
+            (z == 0, 0, 2 * third), (z == last, third, D), ((z > 0) & (z < last), 0, D),
+        ):
+            @pl.when(when)
+            def _(first=first, end=end):
+                turn_slabs(ref, out, slabs, first, end)
+
+    def turn_rest(ref, out, slabs):
+        for when, first, end in ((z == 0, 2 * third, D), (z == last, 0, third)):
+            @pl.when(when)
+            def _(first=first, end=end):
+                turn_slabs(ref, out, slabs, first, end)
+
+    def turn_down(shard):
+        copy = pltpu.make_async_copy(f_down.at[at(shard * deep, deep), :], stage_down, stage_sem.at[2])
+        copy.start()
+        copy.wait()
+
+        def step(i, carry):
+            t_down[at(i * TILE, TILE), at(shard * deep, deep)] = stage_down[:, at(i * TILE, TILE)].T
+            return carry
+
+        lax.fori_loop(0, D // TILE, step, 0)
 
     def saves(m):
         lanes = at(m * toks, toks)
         pairs = (
-            (s_normed, o_normed.at[:, lanes]),
-            (s_context, o_context.at[:, lanes]),
-            (s_second, o_second.at[:, lanes]),
-            (s_inner, o_inner.at[:, lanes]),
-            (s_x, o_x.at[m]),
-            (s_q, o_q.at[m]),
-            (s_kv.at[m], o_kv.at[m]),
-            (s_att, o_att.at[m]),
-            (s_lse, o_lse.at[m]),
-            (s_hidden, o_hidden.at[m]),
-            (s_gu, o_gu.at[m]),
+            (s_normed, o_normed.at[:, lanes]), (s_context, o_context.at[:, lanes]),
+            (s_second, o_second.at[:, lanes]), (s_inner, o_inner.at[:, lanes]),
+            (s_x, o_x.at[m]), (s_q, o_q.at[m]), (s_kv.at[m], o_kv.at[m]), (s_att, o_att.at[m]),
+            (s_lse, o_lse.at[m]), (s_hidden, o_hidden.at[m]), (s_gu, o_gu.at[m]),
         )
         return [pltpu.make_async_copy(a, b, save_sem.at[i]) for i, (a, b) in enumerate(pairs)]
 
     def result_save(m):
         return pltpu.make_async_copy(s_result, o_result.at[m], save_sem.at[11])
 
-    def x_copy(m):
-        return remote(x_in.at[m], x_in.at[m], x_send.at[m], x_recv.at[m], {"section": 1})
+    def x_copy(m, i):
+        part = x_in.at[m, at(i * TILE, TILE), :]
+        return remote(part, part, x_send.at[m, i], x_recv.at[m, i], {"section": 1})
 
     def kv_copy(m, source, slot, lane, to):
         return remote(
@@ -896,8 +934,8 @@
 
     def kv_sends(m):
         return (
+            (0, kv_copy(m, 0, 2, 1, 2)),
             (0, kv_copy(m, 0, 1, 0, 1)),
-            (0, kv_copy(m, 0, 2, 1, 2)),
             (1, kv_copy(m, 0, 2, 0, 3)),
             (2, kv_copy(m, 0, 1, 0, 3)),
         )
@@ -937,54 +975,46 @@
                 value = value + s_att[out_rows, :] * keep[:, lanes]
             s_att[out_rows, :] = value
 
-    def micro(m, carry):
-        @pl.when(m > 0)
-        def _():
-            for save in saves(m - 1):
-                save.wait()
-
-            @pl.when(section == 1)
-            def _():
-                result_save(m - 1).wait()
-
-        @pl.when(section == 0)
-        def _():
-            x_now[...] = ends[m].astype(F32).T
-
-        @pl.when(section == 1)
-        def _():
-            x_copy(m).wait_recv()
-            x_now[...] = x_in[m].astype(F32)
-
-        fill_bias(bias, seg_row, seg_col, m, place, toks)
+    def each(m, blocks, fresh):
+        def step(kv_at, carry):
+            attend(kv_at, m, blocks, fresh)
+            return carry
+
+        lax.fori_loop(0, KV_HEADS, step, 0)
+
+    def take_own(m):
+        x_now[...] = ends[m].astype(F32).T
+
+    def take_sent(m):
+        for i in range(D // TILE):
+            x_copy(m, i).wait_recv()
+        x_now[...] = x_in[m].astype(F32)
+
+    def first_norm(m):
         x = x_now[...]
         s_x[...] = x.astype(LOW)
-        s_normed[...] = (x * column_scale(x) * gains[:, 0:1]).astype(LOW)
-
-        @pl.when(m == 0)
-        def _():
-            loads[0].wait()
-
+        s_normed[...] = (x * column_scale(x) * columns[:, 0:1]).astype(LOW)
+        fill_bias(bias, segments, m, place, toks)
+
+    def rotated(block, head):
         cos, sin = cosine[...], sine[...]
-
-        def rotated(block, head):
-            front = block[head * HEAD : head * HEAD + HALF]
-            back = block[head * HEAD + HALF : (head + 1) * HEAD]
-            return jnp.concatenate([front * cos - back * sin, back * cos + front * sin], axis=0)
-
-        keys = dot(v_joint[:, D : D + KVW], s_normed[...], 0, 0)
+        front = block[head * HEAD : head * HEAD + HALF]
+        back = block[head * HEAD + HALF : (head + 1) * HEAD]
+        return jnp.concatenate([front * cos - back * sin, back * cos + front * sin], axis=0)
+
+    def keys_values(m):
+        keys = dot(t_joint[D : D + KVW, :], s_normed[...], 1, 0)
         for head in range(KV_HEADS):
             s_kv[m, 0, head * HEAD : (head + 1) * HEAD, :] = rotated(keys, head).astype(LOW)
-        s_kv[m, 0, KVW : 2 * KVW, :] = dot(
-            v_joint[:, D + KVW : qkv], s_normed[...], 0, 0
-        ).astype(LOW)
+        s_kv[m, 0, KVW : 2 * KVW, :] = dot(t_joint[D + KVW : qkv, :], s_normed[...], 1, 0).astype(LOW)
         for who, copy in kv_sends(m):
             @pl.when(place == who)
             def _(copy=copy):
                 copy.start()
 
+    def queries(m):
         def query_tile(i, carry):
-            block = dot(v_joint[:, at(i * TILE, TILE)], s_normed[...], 0, 0) * SCALE
+            block = dot(t_joint[at(i * TILE, TILE), :], s_normed[...], 1, 0) * SCALE
             for head in range(TILE // HEAD):
                 rows = at((i * (TILE // HEAD // GROUP) + head // GROUP) * HEAD, HEAD, 64)
                 g = head % GROUP
@@ -993,40 +1023,38 @@
 
         lax.fori_loop(0, D // TILE, query_tile, 0)
 
-        def each(blocks, fresh):
-            def step(kv_at, carry):
-                attend(kv_at, m, blocks, fresh)
-                return carry
-
-            lax.fori_loop(0, KV_HEADS, step, 0)
-
-        each((0,), True)
-
+    def near_block(m):
+        each(m, (0,), True)
+
+    def far_blocks(m):
         @pl.when(place == 1)
         def _():
             kv_copy(m, 0, 1, 0, 1).wait_recv()
-            each((1,), False)
+            each(m, (1,), False)
 
         @pl.when(place == 2)
         def _():
             kv_copy(m, 0, 2, 0, 2).wait_recv()
-            each((2,), False)
+            each(m, (2,), False)
             kv_copy(m, 0, 1, 0, 2).wait_recv()
-            each((1,), False)
+            each(m, (1,), False)
 
         @pl.when(place == 3)
         def _():
+            kv_copy(m, 0, 1, 0, 3).wait_recv()
+            each(m, (1,), False)
             kv_copy(m, 0, 2, 0, 3).wait_recv()
             kv_copy(m, 2, 1, 0, 2).start()
-            kv_copy(m, 0, 1, 0, 3).wait_recv()
-            each((1, 2), False)
-
+            each(m, (2,), False)
+
+    def contexts(m):
         def finish(kv_at, carry):
             one = pl.ds(kv_at, 1)
             total = s_lse[one, :]
+            inverse = 1.0 / total
             for g in range(GROUP):
                 rows = at((kv_at * GROUP + g) * HEAD, HEAD, 64)
-                value = s_att[rows, :] / total[:, g * toks : (g + 1) * toks]
+                value = s_att[rows, :] * inverse[:, g * toks : (g + 1) * toks]
                 s_att[rows, :] = value
                 s_context[rows, :] = value.astype(LOW)
             s_lse[one, :] = s_top[one, :] + jnp.log(total)
@@ -1034,48 +1062,152 @@
 
         lax.fori_loop(0, KV_HEADS, finish, 0)
 
+    def seconds(m):
         def out_tile(i, carry):
             rows = at(i * TILE, TILE)
             s_hidden[rows, :] = x_now[rows, :] + dot(
-                v_joint[:, at(qkv + i * TILE, TILE)], s_context[...], 0, 0
+                t_joint[at(qkv + i * TILE, TILE), :], s_context[...], 1, 0
             )
             return carry
 
         lax.fori_loop(0, D // TILE, out_tile, 0)
         hidden = s_hidden[...]
-        s_second[...] = (hidden * column_scale(hidden) * gains[:, 1:2]).astype(LOW)
-
-        @pl.when(m == 0)
-        def _():
-            loads[1].wait()
-
+        s_second[...] = (hidden * column_scale(hidden) * columns[:, 1:2]).astype(LOW)
+
+    def gates(first, end):
         def gate_tile(i, carry):
             rows, up_rows = at(i * WIDE, WIDE), at(FF + i * WIDE, WIDE)
-            gate = dot(v_gate_up[:, rows], s_second[...], 0, 0)
-            up = dot(v_gate_up[:, up_rows], s_second[...], 0, 0)
+            gate = dot(t_gate_up[rows, :], s_second[...], 1, 0)
+            up = dot(t_gate_up[up_rows, :], s_second[...], 1, 0)
             s_gu[rows, :] = gate
             s_gu[up_rows, :] = up
             s_inner[rows, :] = (gate * jax.nn.sigmoid(gate) * up).astype(LOW)
             return carry
 
-        lax.fori_loop(0, FF // WIDE, gate_tile, 0)
-
-        @pl.when(m == 0)
-        def _():
-            loads[2].wait()
-
-        def down_tile(i, carry):
-            rows = at(i * TILE, TILE)
-            value = s_hidden[rows, :] + dot(v_down[:, rows], s_inner[...], 0, 0)
+        lax.fori_loop(first, end, gate_tile, 0)
+
+    def early(work):
+        @pl.when(section == 0)
+        def _():
+            work()
+
+    for j in range(JOINT_CHUNKS):
+        own_sends(j)
+    for copy in own_copies:
+        copy.start()
+    segments[place] = seg_own[...]
+
+    def seg_copy(i):
+        return remote(
+            seg_own, segments.at[place], seg_sem.at[0, i], seg_sem.at[1, i], {"ctx": (place + i) % 4}
+        )
+
+    for i in (1, 2, 3):
+        seg_copy(i).start()
+    gain_columns(gains, columns)
+    early(lambda: take_own(0))
+    for i in (1, 2, 3):
+        seg_copy(i).wait()
+    early(lambda: first_norm(0))
+
+    joint_items = 3 * JOINT_CHUNKS
+    lap = CHUNKS - JOINT_CHUNKS
+    pump(joint_items + 3)
+    for j in range(JOINT_CHUNKS):
+        for d in (1, 2, 3):
+            complete(d, j)
+    own_copies[0].wait_recv()
+    own_copies[1].wait_recv()
+
+    def turn_all(ref, out, slabs):
+        turn_slabs(ref, out, slabs, 0, D)
+
+    turn_all(f_joint, t_joint, (0, 1))
+    pump(joint_items + 4)
+    turn_all(f_joint, t_joint, (2,))
+    pump(joint_items + 5)
+    early(lambda: keys_values(0))
+    pump(joint_items + 6)
+    early(lambda: queries(0))
+    pump(joint_items + lap)
+    early(lambda: near_block(0))
+    pump(joint_items + lap + 5)
+    early(lambda: far_blocks(0))
+    pump(joint_items + lap + 6)
+    early(lambda: contexts(0))
+    early(lambda: seconds(0))
+    pump(joint_items + 2 * lap)
+    own_copies[2].wait_recv()
+    for d in (1, 2):
+        for j in range(JOINT_CHUNKS, first_down):
+            complete(d, j)
+    for p in range(WIDE_CHUNKS):
+        turn_near(f_gate_up, t_gate_up, (p, WIDE_CHUNKS + p))
+        pump(joint_items + 2 * lap + p + 1)
+
+    def turn_downs(d):
+        for j in range(first_down, CHUNKS):
+            complete(d, j)
+        for valid, shard, onward, more in sides(d):
+            @pl.when(valid)
+            def _(shard=shard):
+                turn_down(shard)
+
+    own_copies[3].wait_recv()
+    turn_down(z)
+    pump(joint_items + 3 * lap - 3)
+    turn_downs(1)
+    pump(joint_items + 3 * lap - 2)
+    turn_downs(2)
+    pump(joint_items + 3 * lap - 1)
+    per_slab = SLAB // WIDE
+    for p in range(WIDE_CHUNKS):
+        complete(3, JOINT_CHUNKS + p)
+        turn_rest(f_gate_up, t_gate_up, (p, WIDE_CHUNKS + p))
+        early(lambda p=p: gates(p * per_slab, (p + 1) * per_slab))
+        if p == 0:
+            pump(joint_items + 3 * lap)
+        flush(joint_items + 3 * lap - 2 + p)
+    turn_downs(3)
+
+    def micro(m, carry):
+        @pl.when(m > 0)
+        def _():
+            for save in saves(m - 1):
+                save.wait()
+
+            @pl.when(section == 1)
+            def _():
+                result_save(m - 1).wait()
+
+        @pl.when((section == 1) | (m > 0))
+        def _():
+            @pl.when(section == 0)
+            def _():
+                take_own(m)
+
+            @pl.when(section == 1)
+            def _():
+                take_sent(m)
+
+            first_norm(m)
+            keys_values(m)
+            queries(m)
+            near_block(m)
+            far_blocks(m)
+            contexts(m)
+            seconds(m)
+            gates(0, FF // WIDE)
+
+        for i in range(D // TILE):
+            rows = slice(i * TILE, (i + 1) * TILE)
+            value = s_hidden[rows, :] + dot(t_down[rows, :], s_inner[...], 1, 0)
             x_now[rows, :] = value
-            x_in[m, rows, :] = value.astype(LOW)
-            return carry
-
-        lax.fori_loop(0, D // TILE, down_tile, 0)
-
-        @pl.when(section == 0)
-        def _():
-            x_copy(m).start()
+
+            @pl.when(section == 0)
+            def _(i=i, rows=rows, value=value):
+                x_in[m, rows, :] = value.astype(LOW)
+                x_copy(m, i).start()
 
         for save in saves(m):
             save.start()
@@ -1088,8 +1220,11 @@
         return carry
 
     lax.fori_loop(0, micros, micro, 0)
+    seg_save = pltpu.make_async_copy(segments, o_seg, seg_sem.at[0, 0])
+    seg_save.start()
     for save in saves(micros - 1):
         save.wait()
+    seg_save.wait()
 
     @pl.when(section == 1)
     def _():
@@ -1098,7 +1233,8 @@
     for m in range(2):
         @pl.when(section == 0)
         def _(m=m):
-            x_copy(m).wait_send()
+            for i in range(D // TILE):
+                x_copy(m, i).wait_send()
 
         for who, copy in kv_sends(m):
             @pl.when(place == who)
@@ -1109,14 +1245,36 @@
         def _(m=m):
             kv_copy(m, 2, 1, 0, 2).wait_send()
 
+    for d, j in order:
+        for valid, shard, onward, more in sides(d):
+            @pl.when(valid)
+            def _(shard=shard, onward=onward, more=more):
+                mate_copy(shard, j, y, y_mate, ys, yr).wait_send()
+                mate_copy(shard, j, y, k_mate, cs, cr).wait_send()
+                mate_copy(shard, j, 1 - y, k_mate, es, er).wait_send()
+                if d < 3:
+                    @pl.when(more)
+                    def _():
+                        z_copy(shard, j, onward, False, False).wait_send()
+    for j in range(CHUNKS):
+        @pl.when(z < last)
+        def _(j=j):
+            z_copy(z, j, z + 1, True, False).wait_send()
+
+        @pl.when(z > 0)
+        def _(j=j):
+            z_copy(z, j, z - 1, True, True).wait_send()
+    for copy in own_copies:
+        copy.wait_send()
+
 
 def backward_kernel(
-    ends, gains, cosine, sine, seg_row, seg_col, w_joint, w_gate_up, w_down,
-    i_x, i_q, i_kv, i_att, i_lse, i_hidden, i_gu,
+    ends, gains, cosine, sine, segments, w_joint, w_gate_up, w_down,
+    i_x, i_q, i_kv, i_att, i_lse, i_hidden, i_gu, i_result,
     o_both, o_mixed, o_hidden, o_grad, o_gains, o_result,
     v_joint, v_gate_up, v_down, g_in, g_now, s_x, s_q, s_kv, s_att, s_lse, s_hid, s_gu,
     s_both, s_mixed, s_hidden, s_grad, s_sum, s_context, s_delta, s_dq, s_dkv, kv_out, kv_in,
-    s_gains, s_result, bias,
+    s_gains, s_result, bias, columns,
     w_sem, load_sem, save_sem, kv_send, kv_recv, x_send, x_recv,
 ):
     section = lax.axis_index("section")
@@ -1144,6 +1302,7 @@
     w_loads[0].start()
     greet([{"ctx": (place + i) % 4} for i in (1, 2, 3)] + [{"section": 1 - section}])
     s_gains[...] = jnp.zeros_like(s_gains)
+    gain_columns(gains, columns)
 
     def saves(m):
         lanes = at(m * toks, toks)
@@ -1218,7 +1377,7 @@
             def _():
                 result_save(m - 1).wait()
 
-        fill_bias(bias, seg_row, seg_col, m, place, toks)
+        fill_bias(bias, segments, m, place, toks)
 
         @pl.when(section == 1)
         def _():
@@ -1262,7 +1421,7 @@
 
         lax.fori_loop(0, D // TILE, second_tile, 0)
         now[1].wait()
-        g_now[...] = s_grad[...].astype(F32) + norm_back(s_sum[...], s_hid[...], gains[:, 1:2], 1)
+        g_now[...] = s_grad[...].astype(F32) + norm_back(s_sum[...], s_hid[...], columns[:, 1:2], 1)
         s_hidden[...] = g_now[...].astype(LOW)
 
         @pl.when(m == 0)
@@ -1367,7 +1526,7 @@
 
         lax.fori_loop(0, D // TILE, rest_tile, 0)
         now[6].wait()
-        g_now[...] = g_now[...] + norm_back(s_sum[...], s_x[...].astype(F32), gains[:, 0:1], 0)
+        g_now[...] = g_now[...] + norm_back(s_sum[...], s_x[...].astype(F32), columns[:, 0:1], 0)
 
         @pl.when(section == 1)
         def _():
@@ -1411,39 +1570,43 @@
                 copy.wait_send()
 
 
-def run_forward(ends, gains, cosine, sine, seg_row, seg_col, joint, gate_up, down):
+def run_forward(ends, gains, cosine, sine, seg_own, w_qkv, w_out, w_gate_up, w_down):
     micros, toks = ends.shape[0], ends.shape[1]
     width = GROUP * toks
     vm, hbm = pl.BlockSpec(memory_space=pltpu.VMEM), pl.BlockSpec(memory_space=pl.ANY)
     sem = pltpu.SemaphoreType.DMA
+    joint = w_qkv.shape[1] + w_out.shape[1]
     outs = [
+        ((D, joint), LOW), ((D, 2 * FF), LOW), ((FF, D), LOW), ((4, micros, toks), jnp.int32),
         ((D, micros * toks), LOW), ((D, micros * toks), LOW), ((D, micros * toks), LOW),
         ((FF, micros * toks), LOW), ((micros, D, toks), LOW), ((micros, KVW, width), LOW),
         ((micros, 3, 2 * KVW, toks), LOW), ((micros, D, toks), F32), ((micros, 8, width), F32),
         ((micros, D, toks), F32), ((micros, 2 * FF, toks), F32), ((micros, toks, D), F32),
     ]
     scratch = [
-        (joint.shape, LOW), (gate_up.shape, LOW), (down.shape, LOW),
+        ((joint, D), LOW), ((2 * FF, D), LOW), ((D, FF), LOW), ((2, D, SLAB), LOW), (w_down.shape, LOW),
         ((micros, D, toks), LOW), ((D, toks), F32),
         ((D, toks), LOW), ((D, toks), LOW), ((D, toks), LOW), ((FF, toks), LOW), ((D, toks), LOW),
         ((KVW, width), LOW), ((micros, 3, 2 * KVW, toks), LOW), ((D, toks), F32), ((8, width), F32),
         ((8, width), F32), ((D, toks), F32), ((2 * FF, toks), F32), ((toks, D), F32), ((3, toks, toks), F32),
+        ((4, micros, toks), jnp.int32), ((D, 2), F32),
     ]
     return pl.pallas_call(
         forward_kernel,
         out_shape=tuple(jax.ShapeDtypeStruct(s, t) for s, t in outs),
-        in_specs=[vm] * 6 + [hbm] * 3,
+        in_specs=[vm] * 5 + [hbm] * 4,
         out_specs=(hbm,) * len(outs),
         scratch_shapes=[pltpu.VMEM(s, t) for s, t in scratch]
-        + [sem((3,)), sem((12,)), sem((micros, 2)), sem((micros, 3)), sem((micros,)), sem((micros,))],
+        + [sem((3,)), sem((2, 4)), sem((12,)), sem((micros, 2)), sem((micros, 3)), sem((micros, 3)), sem((micros, 3))]
+        + [sem((2, 4)), sem((CHUNKS,))] + [sem((4, CHUNKS))] * 8,
         compiler_params=pltpu.CompilerParams(
             collective_id=3, has_side_effects=True, vmem_limit_bytes=62 * 2**20
         ),
         name="layer_forward",
-    )(ends, gains, cosine, sine, seg_row, seg_col, joint, gate_up, down)
-
-
-def run_backward(ends, gains, cosine, sine, seg_row, seg_col, joint, gate_up, down, saved):
+    )(ends, gains, cosine, sine, seg_own, w_qkv, w_out, w_gate_up, w_down)
+
+
+def run_backward(ends, gains, cosine, sine, segments, joint, gate_up, down, saved):
     micros, toks = ends.shape[0], ends.shape[1]
     width = GROUP * toks
     vm, hbm = pl.BlockSpec(memory_space=pltpu.VMEM), pl.BlockSpec(memory_space=pl.ANY)
@@ -1461,20 +1624,21 @@
         ((2 * FF, toks), LOW), ((qkv, toks), LOW), ((D, toks), LOW), ((D, toks), LOW), ((D, toks), F32),
         ((KVW, width), LOW), ((8, width), F32), ((KVW, width), F32), ((2 * KVW, toks), F32),
         ((micros, 2, 2 * KVW, toks), LOW), ((micros, 2, 2 * KVW, toks), LOW),
-        ((2, D, 128), F32), ((toks, D), F32), ((3, toks, toks), F32),
+        ((2, D, 128), F32), ((toks, D), F32), ((3, toks, toks), F32), ((D, 2), F32),
     ]
     return pl.pallas_call(
         backward_kernel,
         out_shape=tuple(jax.ShapeDtypeStruct(s, t) for s, t in outs),
-        in_specs=[vm] * 6 + [hbm] * 10,
+        in_specs=[vm] * 5 + [hbm] * 11,
         out_specs=(hbm,) * len(outs),
         scratch_shapes=[pltpu.VMEM(s, t) for s, t in scratch]
         + [sem((3,)), sem((7,)), sem((6,)), sem((micros, 2)), sem((micros, 2)), sem((micros,)), sem((micros,))],
         compiler_params=pltpu.CompilerParams(
             collective_id=4, has_side_effects=True, vmem_limit_bytes=62 * 2**20
         ),
+        input_output_aliases={15: 5},
         name="layer_backward",
-    )(ends, gains, cosine, sine, seg_row, seg_col, joint, gate_up, down, *saved)
+    )(ends, gains, cosine, sine, segments, joint, gate_up, down, *saved)
 
 
 def small_mesh():
@@ -1500,35 +1664,26 @@
 
 
 def local_small(ends, segment_ids, w_qkv, w_out, w_gate_up, w_down, gains):
-    section_index = lax.axis_index("section")
     tok_rows = ends.shape[3]
     local_ends = ends[0, :, 0]
     seg_local = segment_ids[:, 0]
-    seg_whole = lax.all_gather(seg_local, "ctx", axis=1, tiled=True)
     query_pos = lax.axis_index("ctx") * tok_rows + jnp.arange(tok_rows, dtype=jnp.int32)
     frequency = 10000.0 ** (-(jnp.arange(HEAD // 2).astype(jnp.float32) * 2.0 / HEAD))
     angle_table = frequency[:, None] * query_pos.astype(jnp.float32)[None, :]
-    shared = (
-        local_ends,
-        gains[0].T,
-        jnp.cos(angle_table),
-        jnp.sin(angle_table),
-        seg_local[:, None, :],
-        seg_whole[:, :, None],
-    ) + tuple(gather_weights(jnp.concatenate([w_qkv[0], w_out[0]], axis=1), w_gate_up[0], w_down[0]))
-    normed, context, second, inner, *saved, result = run_forward(*shared)
-    x, q, kv, att, lse, hidden, gate_up = saved
-    both, mixed, hidden_low, grad, gain_parts, input_grads = run_backward(
-        *shared, (x, q, kv, att, lse, hidden, gate_up)
+    shared = (local_ends, gains[0], jnp.cos(angle_table), jnp.sin(angle_table))
+    joint, gate_up, down, segments, normed, context, second, inner, *saved, result = run_forward(
+        *shared, seg_local, w_qkv[0], w_out[0], w_gate_up[0], w_down[0]
+    )
+    both, mixed, hidden_low, grad, gain_parts, ends_rows = run_backward(
+        *shared, segments, joint, gate_up, down, (*saved, result)
     )
     gain_rows = jnp.sum(gain_parts, axis=-1).reshape(2, 16, D // 16)
     gain_tiles = jnp.pad(jnp.swapaxes(gain_rows, 0, 1), ((0, 0), (0, 6), (0, 128 - D // 16)))
     g_down, g_gate_up, g_qkv, g_out, gain = reduce_grads(
         (normed, context, second, inner), (both, mixed, hidden_low, grad), gain_tiles
     )
-    ends_out = jnp.where(section_index == 0, input_grads, result)[None, :, None]
     return (
-        ends_out, g_qkv[None], g_out[None], g_gate_up[None], g_down[None],
+        ends_rows[None, :, None], g_qkv[None], g_out[None], g_gate_up[None], g_down[None],
         gain[None, :2, : D // 16],
     )
 

time: 549 us -> 549 us (level); the launches traced: 549 us -> 540 us
  blocking collectives: 6.43 us -> 0 us
    pallas_call x1, Pallas kernels: 49.7 us -> 194 us  [run_forward(): pl.pallas_call(forward_kernel, out_shape=tuple((jax.ShapeDtypeStruct(s, t...]
    pallas_call x1 -> x0, Pallas kernels: 135 us -> none  [gather_weights(): pl.pallas_call(gather_kernel, out_shape=tuple((jax.ShapeDtypeStruct((size...]
    pallas_call x1, Pallas kernels: 164 us -> 157 us  [run_backward(): pl.pallas_call(backward_kernel, out_shape=tuple((jax.ShapeDtypeStruct(s,...]
    all_gather x1 -> x0, blocking collectives: 6.43 us -> none  [local_small(): seg_whole = lax.all_gather(seg_local, 'ctx', axis=1, tiled=True)]
where the time goes in v1:
time: 549 us; the launch traced here: 540 us
  Pallas kernels  526 us (96%)
  local copies, waits for them, and re-layouts  10.3 us (2%)
    pallas_call x1, Pallas kernels, run_forward(): pl.pallas_call(forward_kernel, out_shape=tuple((jax.ShapeDtypeStruct(s, t...  194 us
    pallas_call x1, Pallas kernels, reduce_grads(): pl.pallas_call(reduce_kernel, out_shape=tuple((jax.ShapeDtypeStruct(s, f3...  175 us
    pallas_call x1, Pallas kernels, run_backward(): pl.pallas_call(backward_kernel, out_shape=tuple((jax.ShapeDtypeStruct(s,...  157 us

profile of v1, /device:TPU:0, one launch (start us, length us, event | category | flops | bytes accessed | tf_op | source)
XLA Modules:
  0.0 540.3 jit_solution(3637521010301274115)
XLA Ops:
  0.7 1.3 copy.21
  1.9 0.8 multiply_sine_fusion
  2.7 194.3 %layer_forward.1 = (bf16[1152,3072]{1,0:T(8,128)(2,1)}, bf16[1152,6144]{1,0:T(8,128)(2,1)}, bf16[3072,1152]{1,0:T(8,128)(2,1)}, s32[4,2,256]{2,1,0:T(2,128)}, bf...) custom-call(bf16[2,256,1152]{2,1,0:T(8,128)(2,1)} %bitcast.22, ...), custom_call_target="tpu_custom_call" | custom-call | tf_op jit(solution)/shard_map/layer_forward/pallas_call | solution.py:1594
  197.0 157.0 %layer_backward.1 = (bf16[6144,512]{1,0:T(8,128)(2,1)}, bf16[1920,512]{1,0:T(8,128)(2,1)}, bf16[1152,512]{1,0:T(8,128)(2,1)}, bf16[1152,512]{1,0:T(8,128)(2,1)},...) custom-call(bf16[2,256,1152]{2,1,0:T(8,128)(2,1)} %bitcast.23, ...), custom_call_target="tpu_custom_call", output_to_operand_aliasing={{5}: (15, {})} | custom-call | tf_op jit(solution)/shard_map/layer_backward/pallas_call | solution.py:1629
  354.1 1.7 reduce_sum.9
  355.8 0.1 reshape.27
  355.9 0.6 pad.4.gain_tiles
  356.5 174.9 %grads_reduce.1 = (f32[192,1152]{1,0:T(8,128)}, f32[72,6144]{1,0:T(8,128)}, f32[72,1920]{1,0:T(8,128)}, f32[72,1152]{1,0:T(8,128)}, f32[8,128]{1,0:T(8,128)}) custom-call(bf16[3072,512]{1,0:T(8,128)(2,1)} %get-tuple-element.46.inner_h, bf16[1152,512]{1,0:T(8,128)(2,1)} %get-tuple-element.47.grad_h, bf16[1152,512]{1,0:T(8,128)(2,1)} %get-tuple-element.48.second_h, ...), custom_call_target="tpu_custom_call" | custom-call | tf_op jit(solution)/shard_map/grads_reduce/pallas_call | solution.py:639
  531.5 1.2 slice_bitcast_fusion
  532.7 0.0 copy-start.2
  532.7 0.0 copy-start.3
  532.7 3.3 copy.28
  536.0 0.0 copy-done.2
  536.0 0.0 copy-start
  536.0 0.8 copy.29
  536.8 0.0 copy-done.3
  536.8 0.0 copy-start.1
  536.8 0.7 copy.30
  537.6 0.1 copy-done
  537.7 1.2 copy.31
  538.9 0.0 copy-done.1
  538.9 0.9 copy.32
  (3 shorter events, 0.0 us)
Async XLA Ops:
  532.7 3.3 copy-start.2
  532.7 4.1 copy-start.3
  536.0 1.7 copy-start
  536.8 2.1 copy-start.1

commit v2 on v1

--- a/solution.py
+++ b/solution.py
@@ -330,321 +330,9 @@
 DOWN_COLS = 128
 WIDE_COLS = 384
 NEAR, MID, FAR, SUMS = 2, 4, 8, 12
-
-
-def reduce_kernel(
-    inner_h, grad_h, second_h, both_h, normed_h, mixed_h, context_h, hidden_h, gain_tiles,
-    o_down, o_gate_up, o_qkv, o_out, o_gain,
-    *scratch,
-):
-    kinds = (scratch[0:9], scratch[9:18])
-    (near_send, near_recv, mid_send, mid_recv, right_send, right_recv, left_send, left_recv,
-     near_free, mid_free, right_free, left_free) = scratch[18:30]
-    operands, load_sem, gain_in, gain_send, gain_recv = scratch[30:38], *scratch[38:42]
-    inner_t, g_low, second_t, both, normed_t, mixed, context_t, hidden_low = operands
-    loads = [
-        pltpu.make_async_copy(src, dst, load_sem.at[i])
-        for i, (src, dst) in enumerate(
-            zip((inner_h, grad_h, second_h, both_h, normed_h, mixed_h, context_h, hidden_h), operands)
-        )
-    ]
-    for load in loads:
-        load.start()
-    place = lax.axis_index("ctx")
-    z = lax.axis_index("fsdp")
-    last = lax.axis_size("fsdp") - 1
-    y, k = place // 2, place % 2
-    y_mate = {"ctx": (1 - y) * 2 + k}
-    k_mate = {"ctx": y * 2 + 1 - k}
-    right, left = {"fsdp": z + 1}, {"fsdp": z - 1}
-    f32, low = jnp.float32, jnp.bfloat16
-
-    n_down = g_low.shape[0] // DOWN_COLS
-    n_both = both.shape[0] // WIDE_COLS
-    n_mixed = mixed.shape[0] // WIDE_COLS
-    n_out = hidden_low.shape[0] // WIDE_COLS
-    end_both = n_down + n_both
-    end_mixed = end_both + n_mixed
-    total = end_mixed + n_out
-    hop = 2
-    first_z = 3
-    final_lag = first_z + hop * 3
-
-    barrier = pltpu.get_barrier_semaphore()
-    me = place * 4 + z
-    others = [((place + i // 4) % 4, (z + i % 4) % 4) for i in range(1, 16)]
-    for to_place, to_z in others:
-        pl.semaphore_signal(barrier, inc=1, device_id={"ctx": to_place, "fsdp": to_z}, device_id_type=MESH)
-    pl.semaphore_wait(barrier, 15)
-
-    def gain_copy(i):
-        to_place, to_z = others[i - 1]
-        return pltpu.make_async_remote_copy(
-            src_ref=gain_tiles.at[to_place * 4 + to_z], dst_ref=gain_in.at[i],
-            send_sem=gain_send.at[i], recv_sem=gain_recv.at[i],
-            device_id={"ctx": to_place, "fsdp": to_z}, device_id_type=MESH)
-
-    for i in range(1, 16):
-        gain_copy(i).start()
-
-    def typed(j, work):
-        @pl.when((j >= 0) & (j < n_down))
-        def _():
-            work(0)
-
-        @pl.when((j >= n_down) & (j < total))
-        def _():
-            work(1)
-
-    def near_copy(kind, j):
-        out_near, own_near, in_near = kinds[kind][0:3]
-        slot = j % NEAR
-        return pltpu.make_async_remote_copy(
-            src_ref=out_near.at[slot], dst_ref=in_near.at[slot], send_sem=near_send.at[slot],
-            recv_sem=near_recv.at[slot], device_id=k_mate, device_id_type=MESH)
-
-    def mid_copy(kind, j):
-        out_mid, in_mid = kinds[kind][3:5]
-        slot = j % MID
-        return pltpu.make_async_remote_copy(
-            src_ref=out_mid.at[slot], dst_ref=in_mid.at[slot], send_sem=mid_send.at[slot],
-            recv_sem=mid_recv.at[slot], device_id=y_mate, device_id_type=MESH)
-
-    def line_rows(kind, step, rightward):
-        rows = kinds[kind][5].shape[1]
-        part = rows // 4
-        if rightward:
-            start = (part * (step + 1)) // 16 * 16
-            return start, rows - start
-        return 0, (part * step + 15) // 16 * 16
-
-    def line_copy(kind, j, step, rightward):
-        start, count = line_rows(kind, step, rightward)
-        src, dst = (kinds[kind][6], kinds[kind][7]) if rightward else (kinds[kind][6], kinds[kind][8])
-        lane = 0 if rightward else 1
-        return pltpu.make_async_remote_copy(
-            src_ref=src.at[lane, j % NEAR, pl.ds(start, count), :],
-            dst_ref=dst.at[j % FAR, pl.ds(start, count), :],
-            send_sem=(right_send if rightward else left_send).at[j % NEAR],
-            recv_sem=(right_recv if rightward else left_recv).at[j % FAR],
-            device_id=right if rightward else left, device_id_type=MESH)
-
-    def multiply(kind, j, lhs, rhs, first, cols):
-        out_near, own_near = kinds[kind][0:2]
-        slot = j % NEAR
-        rows = own_near.shape[2]
-        columns = pl.ds(pl.multiple_of((j - first) * cols, 128), cols)
-        block = rhs[columns, :]
-        for yy in range(2):
-            for mine in (False, True):
-                kk = k if mine else 1 - k
-                at = pl.ds(pl.multiple_of((yy * 2 + kk) * rows, 16), rows)
-                part = lax.dot_general(lhs[at, :], block, (((1,), (1,)), ((), ())), preferred_element_type=f32)
-                (own_near if mine else out_near)[slot, yy] = part.astype(low)
-
-    def stage_near(j):
-        for i, first in enumerate((0, n_down, end_both, end_mixed)):
-            @pl.when(j == first)
-            def _(i=i):
-                loads[2 * i].wait()
-                loads[2 * i + 1].wait()
-
-        @pl.when((j >= NEAR) & (j < total))
-        def _():
-            typed(j - NEAR, lambda kind: near_copy(kind, j - NEAR).wait_send())
-
-        @pl.when(j < n_down)
-        def _():
-            multiply(0, j, inner_t, g_low, 0, DOWN_COLS)
-
-        @pl.when((j >= n_down) & (j < end_both))
-        def _():
-            multiply(1, j, second_t, both, n_down, WIDE_COLS)
-
-        @pl.when((j >= end_both) & (j < end_mixed))
-        def _():
-            multiply(1, j, normed_t, mixed, end_both, WIDE_COLS)
-
-        @pl.when((j >= end_mixed) & (j < total))
-        def _():
-            multiply(1, j, context_t, hidden_low, end_mixed, WIDE_COLS)
-
-        @pl.when((j >= NEAR) & (j < total))
-        def _():
-            pl.semaphore_wait(near_free, 1)
-
-        typed(j, lambda kind: near_copy(kind, j).start())
-
-    def stage_mid(j):
-        def work(kind):
-            out_near, own_near, in_near, out_mid, in_mid, sums = kinds[kind][0:6]
-            near_copy(kind, j).wait_recv()
-            slot = j % NEAR
-            out_mid[j % MID] = (own_near[slot, 1 - y].astype(f32) + in_near[slot, 1 - y].astype(f32)).astype(low)
-            sums[j % SUMS] = own_near[slot, y].astype(f32) + in_near[slot, y].astype(f32)
-
-        @pl.when((j >= MID) & (j < total))
-        def _():
-            typed(j - MID, lambda kind: mid_copy(kind, j - MID).wait_send())
-
-        typed(j, work)
-
-        @pl.when((j >= 0) & (j + NEAR < total))
-        def _():
-            pl.semaphore_signal(near_free, inc=1, device_id=k_mate, device_id_type=MESH)
-
-        @pl.when((j >= MID) & (j < total))
-        def _():
-            pl.semaphore_wait(mid_free, 1)
-
-        typed(j, lambda kind: mid_copy(kind, j).start())
-
-    def stage_sum(j):
-        def work(kind):
-            in_mid, sums = kinds[kind][4:6]
-            mid_copy(kind, j).wait_recv()
-            sums[j % SUMS] = sums[j % SUMS] + in_mid[j % MID].astype(f32)
-
-        typed(j, work)
-
-        @pl.when((j >= 0) & (j + MID < total))
-        def _():
-            pl.semaphore_signal(mid_free, inc=1, device_id=y_mate, device_id_type=MESH)
-
-    def stage_line(i, rightward):
-        free = right_free if rightward else left_free
-        for at in range(4):
-            step = at if rightward else 3 - at
-            if step == 3:
-                continue
-            j = i - first_z - hop * step
-
-            @pl.when((z == at) & (j >= 0) & (j < total))
-            def _(at=at, step=step, j=j):
-                @pl.when(j >= NEAR)
-                def _():
-                    typed(j - NEAR, lambda kind: line_copy(kind, j - NEAR, at, rightward).wait_send())
-
-                def work(kind):
-                    sums, out_line, in_right, in_left = kinds[kind][5:9]
-                    start, count = line_rows(kind, at, rightward)
-                    rows = pl.ds(start, count)
-                    value = sums[j % SUMS, rows, :]
-                    if step > 0:
-                        came = line_rows(kind, at - 1 if rightward else at + 1, rightward)
-                        arrive = line_copy(kind, j, at - 1 if rightward else at + 1, rightward)
-                        arrive.wait_recv()
-                        value = value + (in_right if rightward else in_left)[j % FAR, rows, :].astype(f32)
-                    out_line[0 if rightward else 1, j % NEAR, rows, :] = value.astype(low)
-
-                typed(j, work)
-
-                @pl.when(j >= FAR)
-                def _():
-                    pl.semaphore_wait(free, 1)
-
-                typed(j, lambda kind: line_copy(kind, j, at, rightward).start())
-
-    def store(kind, j, value):
-        if kind == 0:
-            o_down[:, pl.ds(pl.multiple_of(j * DOWN_COLS, 128), DOWN_COLS)] = value
-            return
-        for out, first, end in ((o_gate_up, n_down, end_both), (o_qkv, end_both, end_mixed), (o_out, end_mixed, total)):
-            @pl.when((j >= first) & (j < end))
-            def _(out=out, first=first):
-                out[:, pl.ds(pl.multiple_of((j - first) * WIDE_COLS, 128), WIDE_COLS)] = value
-
-    def stage_final(j):
-        for at in range(4):
-            @pl.when((z == at) & (j >= 0) & (j < total))
-            def _(at=at):
-                def work(kind):
-                    sums, out_line, in_right, in_left = kinds[kind][5:9]
-                    part = sums.shape[1] // 4
-                    if at == 3:
-                        line_copy(kind, j, 2, True).wait_recv()
-                    if at == 0:
-                        line_copy(kind, j, 1, False).wait_recv()
-                    low_at = at * part // 16 * 16
-                    high_at = (at * part + part + 15) // 16 * 16
-                    rows = pl.ds(low_at, high_at - low_at)
-                    value = sums[j % SUMS, rows, :]
-                    if at > 0:
-                        value = value + in_right[j % FAR, rows, :].astype(f32)
-                    if at < 3:
-                        value = value + in_left[j % FAR, rows, :].astype(f32)
-                    shift = at * part - low_at
-                    store(kind, j, value[shift:shift + part])
-
-                typed(j, work)
-                if at > 0:
-                    @pl.when(j + FAR < total)
-                    def _():
-                        pl.semaphore_signal(right_free, inc=1, device_id=left, device_id_type=MESH)
-                if at < 3:
-                    @pl.when(j + FAR < total)
-                    def _():
-                        pl.semaphore_signal(left_free, inc=1, device_id=right, device_id_type=MESH)
-
-    def iteration(i, carry):
-        stage_near(i)
-        stage_mid(i - 1)
-        stage_sum(i - 3)
-        stage_line(i, True)
-        stage_line(i, False)
-        stage_final(i - final_lag)
-        return carry
-
-    lax.fori_loop(0, total + final_lag, iteration, 0)
-    gain = gain_tiles[me]
-    for i in range(1, 16):
-        gain_copy(i).wait()
-        gain = gain + gain_in[i]
-    o_gain[...] = gain
-    for j in range(total - NEAR, total):
-        near_copy(1, j).wait_send()
-        for at in range(3):
-            @pl.when(z == at)
-            def _(at=at):
-                line_copy(1, j, at, True).wait_send()
-
-            @pl.when(z == at + 1)
-            def _(at=at):
-                line_copy(1, j, at + 1, False).wait_send()
-    for j in range(total - MID, total):
-        mid_copy(1, j).wait_send()
-
-
-def reduce_grads(lefts, rights, gain_tiles):
-    normed, context, second, inner = lefts
-    both, mixed, hidden, grad = rights
-    ops = (inner, grad, second, both, normed, mixed, context, hidden)
-    low, f32 = jnp.bfloat16, jnp.float32
-    scratch = []
-    for rows, cols in ((inner.shape[0] // 4, DOWN_COLS), (second.shape[0] // 4, WIDE_COLS)):
-        scratch += [
-            pltpu.VMEM((NEAR, 2, rows, cols), low), pltpu.VMEM((NEAR, 2, rows, cols), low), pltpu.VMEM((NEAR, 2, rows, cols), low),
-            pltpu.VMEM((MID, rows, cols), low), pltpu.VMEM((MID, rows, cols), low),
-            pltpu.VMEM((SUMS, rows, cols), f32),
-            pltpu.VMEM((2, NEAR, rows, cols), low),
-            pltpu.VMEM((FAR, rows, cols), low), pltpu.VMEM((FAR, rows, cols), low)]
-    sem = pltpu.SemaphoreType
-    scratch += [sem.DMA((NEAR,)), sem.DMA((NEAR,)), sem.DMA((MID,)), sem.DMA((MID,)),
-                sem.DMA((NEAR,)), sem.DMA((FAR,)), sem.DMA((NEAR,)), sem.DMA((FAR,)),
-                sem.REGULAR, sem.REGULAR, sem.REGULAR, sem.REGULAR]
-    scratch += [pltpu.VMEM(op.shape, low) for op in ops]
-    scratch += [sem.DMA((8,)), pltpu.VMEM((16, 8, 128), f32), sem.DMA((16,)), sem.DMA((16,))]
-    outs = [(a.shape[0] // 16, b.shape[0]) for a, b in zip(ops[0::2], ops[1::2])] + [(8, 128)]
-    vm, hbm = pl.BlockSpec(memory_space=pltpu.VMEM), pl.BlockSpec(memory_space=pl.ANY)
-    return pl.pallas_call(
-        reduce_kernel,
-        out_shape=tuple(jax.ShapeDtypeStruct(s, f32) for s in outs),
-        in_specs=[hbm] * 8 + [vm],
-        out_specs=(vm,) * 5,
-        scratch_shapes=scratch,
-        compiler_params=pltpu.CompilerParams(collective_id=2, has_side_effects=True, vmem_limit_bytes=62 * 2**20),
-        name="grads_reduce",
-    )(*ops, gain_tiles)
+OWNERS = 16
+EMBEDDED, DEFERRED = 6, 6
+AHEAD = 4
 
 
 F32, LOW = jnp.float32, jnp.bfloat16
@@ -1079,8 +767,8 @@
             rows, up_rows = at(i * WIDE, WIDE), at(FF + i * WIDE, WIDE)
             gate = dot(t_gate_up[rows, :], s_second[...], 1, 0)
             up = dot(t_gate_up[up_rows, :], s_second[...], 1, 0)
-            s_gu[rows, :] = gate
-            s_gu[up_rows, :] = up
+            s_gu[rows, :] = gate.astype(LOW)
+            s_gu[up_rows, :] = up.astype(LOW)
             s_inner[rows, :] = (gate * jax.nn.sigmoid(gate) * up).astype(LOW)
             return carry
 
@@ -1270,12 +958,14 @@
 
 def backward_kernel(
     ends, gains, cosine, sine, segments, w_joint, w_gate_up, w_down,
-    i_x, i_q, i_kv, i_att, i_lse, i_hidden, i_gu, i_result,
-    o_both, o_mixed, o_hidden, o_grad, o_gains, o_result,
+    i_x, i_q, i_kv, i_att, i_lse, i_hidden, i_gu, i_result, i_normed, i_context, i_second, i_inner,
+    o_result, o_down, o_gate_up, o_qkv, o_out, o_gain,
     v_joint, v_gate_up, v_down, g_in, g_now, s_x, s_q, s_kv, s_att, s_lse, s_hid, s_gu,
     s_both, s_mixed, s_hidden, s_grad, s_sum, s_context, s_delta, s_dq, s_dkv, kv_out, kv_in,
-    s_gains, s_result, bias, columns,
-    w_sem, load_sem, save_sem, kv_send, kv_recv, x_send, x_recv,
+    s_gains, bias, columns, wide_out, down_out, gain_out, gain_in,
+    w_sem, load_sem, gu_sem, save_sem, kv_send, kv_recv, x_send, x_recv,
+    left_sem, near_send, near_recv, mid_send, mid_recv, right_send, right_recv, left_send, left_recv,
+    out_sem, gain_send, gain_recv, near_free, mid_free, right_free, left_free,
 ):
     section = lax.axis_index("section")
     place = lax.axis_index("ctx")
@@ -1290,37 +980,51 @@
 
     def loads(m):
         pairs = (
-            (i_gu, s_gu), (i_hidden, s_hid), (i_att, s_att), (i_q, s_q), (i_kv, s_kv),
+            (i_hidden, s_hid), (i_att, s_att), (i_q, s_q), (i_kv, s_kv),
             (i_lse, s_lse), (i_x, s_x),
         )
         return [pltpu.make_async_copy(a.at[m], b, load_sem.at[i]) for i, (a, b) in enumerate(pairs)]
 
+    tiles = FF // TILE
+
+    def gu_loads(m, i):
+        slot = i % AHEAD
+        return [
+            pltpu.make_async_copy(
+                i_gu.at[m, at(part * FF + i * TILE, TILE), :], s_gu.at[slot, part], gu_sem.at[slot, part]
+            )
+            for part in range(2)
+        ]
+
     w_loads[2].start()
+    for i in range(AHEAD):
+        for load in gu_loads(0, i):
+            load.start()
     for load in loads(0):
         load.start()
     w_loads[1].start()
     w_loads[0].start()
-    greet([{"ctx": (place + i) % 4} for i in (1, 2, 3)] + [{"section": 1 - section}])
+    z = lax.axis_index("fsdp")
+    last = lax.axis_size("fsdp") - 1
+    others = [((place + i // 4) % 4, (z + i % 4) % 4) for i in range(1, OWNERS)]
+    greet([{"ctx": a, "fsdp": b} for a, b in others] + [{"section": 1 - section}])
     s_gains[...] = jnp.zeros_like(s_gains)
     gain_columns(gains, columns)
 
-    def saves(m):
-        lanes = at(m * toks, toks)
-        pairs = (
-            (s_both, o_both.at[:, lanes]), (s_mixed, o_mixed.at[:, lanes]),
-            (s_hidden, o_hidden.at[:, lanes]), (s_grad, o_grad.at[:, lanes]),
-        )
-        return [pltpu.make_async_copy(a, b, save_sem.at[i]) for i, (a, b) in enumerate(pairs)]
-
-    def result_save(m):
-        return pltpu.make_async_copy(s_result, o_result.at[m], save_sem.at[4])
+    def result_saves(m):
+        return [
+            pltpu.make_async_copy(
+                s_dq.at[0:toks, at(i % 2 * TILE, TILE)], o_result.at[m, :, i * TILE : (i + 1) * TILE], save_sem.at[i]
+            )
+            for i in range(D // TILE)
+        ]
 
     def g_copy(m):
         return remote(g_in.at[m], g_in.at[m], x_send.at[m], x_recv.at[m], {"section": 0})
 
     def kv_copy(m, source, slot, lane, to):
         return remote(
-            kv_out.at[m, source], kv_in.at[m, slot], kv_send.at[m, lane], kv_recv.at[m, slot],
+            kv_out.at[source], kv_in.at[m, slot], kv_send.at[m, lane], kv_recv.at[m, slot],
             {"ctx": to},
         )
 
@@ -1356,55 +1060,438 @@
 
         lax.fori_loop(0, KV_HEADS, step, 0)
 
+    y, k = place // 2, place % 2
+    y_mate = {"ctx": (1 - y) * 2 + k}
+    k_mate = {"ctx": y * 2 + 1 - k}
+    right, left = {"fsdp": z + 1}, {"fsdp": z - 1}
+    n_down, n_both = D // DOWN_COLS, 2 * FF // WIDE_COLS
+    n_mixed, n_out = qkv // WIDE_COLS, D // WIDE_COLS
+    end_both = n_down + n_both
+    end_mixed = end_both + n_mixed
+    total = end_mixed + n_out
+    hop, first_z = 2, 4
+    final_lag = first_z + hop * 3
+    block = D // 4
+    parts = (FF // OWNERS // 3, D // OWNERS)
+    used = (4 * parts[0], block)
+    spare = 13 * WIDE_COLS
+    both_toks = micros * toks
+    inner_t = v_down.at[:, 0:both_toks]
+    normed_t = v_down.at[0:D, both_toks : 2 * both_toks]
+    context_t = v_gate_up.at[:, spare : spare + both_toks]
+    second_t = v_gate_up.at[:, spare + both_toks : spare + 2 * both_toks]
+    left_loads = [
+        pltpu.make_async_copy(a, b, left_sem.at[i])
+        for i, (a, b) in enumerate(
+            ((i_inner, inner_t), (i_normed, normed_t), (i_context, context_t), (i_second, second_t))
+        )
+    ]
+
+    def cell(column, slot, first=0, count=block):
+        rows = at(slot % 4 * block + first, count, 16)
+        return v_gate_up.at[rows, at((column + slot // 4) * WIDE_COLS, WIDE_COLS)]
+
+    def out_near(slot, yy):
+        return cell(0, slot * 2 + yy)
+
+    def own_near(slot, yy):
+        return cell(1, slot * 2 + yy)
+
+    def in_near(slot, yy):
+        return cell(2, slot * 2 + yy)
+
+    def gain_copy(i):
+        to_place, to_z = others[i - 1]
+        return remote(
+            gain_out.at[to_place * 4 + to_z], gain_in.at[i], gain_send.at[i], gain_recv.at[i],
+            {"ctx": to_place, "fsdp": to_z},
+        )
+
+    def near_copy(j):
+        slot = j % NEAR
+        return remote(
+            cell(0, slot * 2, 0, 2 * block), cell(2, slot * 2, 0, 2 * block),
+            near_send.at[slot], near_recv.at[slot], k_mate,
+        )
+
+    def mid_copy(kind, j):
+        slot = j % MID
+        return remote(
+            cell(3, slot, 0, used[kind]), cell(4, slot, 0, used[kind]),
+            mid_send.at[slot], mid_recv.at[slot], y_mate,
+        )
+
+    def line_rows(kind, here, rightward):
+        part = parts[kind]
+        if rightward:
+            start = (part * (here + 1)) // 16 * 16
+            return start, used[kind] - start
+        return 0, (part * here + 15) // 16 * 16
+
+    def line_copy(kind, j, here, rightward):
+        start, count = line_rows(kind, here, rightward)
+        lane, slot = (0 if rightward else 1), j % NEAR
+        return remote(
+            cell(8, lane * NEAR + slot, start, count), cell(9 if rightward else 11, j % FAR, start, count),
+            (right_send if rightward else left_send).at[slot],
+            (right_recv if rightward else left_recv).at[j % FAR],
+            right if rightward else left,
+        )
+
+    def out_copy(kind, j, first):
+        slot = j % NEAR
+        if kind == 0:
+            return pltpu.make_async_copy(
+                down_out.at[slot], o_down.at[:, at(j * DOWN_COLS, DOWN_COLS)], out_sem.at[slot]
+            )
+        out = {n_down: o_gate_up, end_both: o_qkv, end_mixed: o_out}[first]
+        return pltpu.make_async_copy(
+            wide_out.at[slot], out.at[:, at((j - first) * WIDE_COLS, WIDE_COLS)], out_sem.at[slot]
+        )
+
+    def out_wait(kind, slot):
+        src, dst = (wide_out, o_out.at[:, 0:WIDE_COLS]) if kind else (down_out, o_down.at[:, 0:DOWN_COLS])
+        pltpu.make_async_copy(src.at[slot], dst, out_sem.at[slot]).wait()
+
+    def open_buffers():
+        pl.semaphore_signal(near_free, inc=NEAR, device_id=k_mate, device_id_type=MESH)
+        pl.semaphore_signal(mid_free, inc=MID, device_id=y_mate, device_id_type=MESH)
+
+        @pl.when(z > 0)
+        def _():
+            pl.semaphore_signal(right_free, inc=FAR, device_id=left, device_id_type=MESH)
+
+        @pl.when(z < last)
+        def _():
+            pl.semaphore_signal(left_free, inc=FAR, device_id=right, device_id_type=MESH)
+
+    def when(condition):
+        if isinstance(condition, bool):
+            return (lambda work: work()) if condition else (lambda work: None)
+        return pl.when(condition)
+
+    def inside(j, first, end):
+        if isinstance(j, int):
+            return first <= j < end
+        return (j >= first) & (j < end)
+
+    def typed(j, work):
+        @when(inside(j, 0, n_down))
+        def _():
+            work(0)
+
+        @when(inside(j, n_down, total))
+        def _():
+            work(1)
+
+    def multiply_down(j):
+        rhs = s_grad[at(j * DOWN_COLS, DOWN_COLS), :]
+        rows, piece = FF // 4, parts[0]
+        for yy in range(2):
+            for mine in (False, True):
+                kk = k if mine else 1 - k
+                lhs = v_down[at((yy * 2 + kk) * rows, rows), 0:both_toks]
+                value = dot(lhs, rhs, 1, 1).astype(LOW)
+                out = (own_near if mine else out_near)(j % NEAR, yy)
+                for zz in range(4):
+                    for t in range(3):
+                        start = (zz * 3 + t) * piece
+                        out[zz * piece : (zz + 1) * piece, t * 128 : (t + 1) * 128] = value[start : start + piece]
+
+    def multiply_wide(j, lhs, rhs, first):
+        right_rows = rhs[at((j - first) * WIDE_COLS, WIDE_COLS), :]
+        for yy in range(2):
+            for mine in (False, True):
+                kk = k if mine else 1 - k
+                value = dot(lhs[at((yy * 2 + kk) * block, block, 16), :], right_rows, 1, 1)
+                (own_near if mine else out_near)(j % NEAR, yy)[...] = value.astype(LOW)
+
+    def stage_near(j):
+        for first, load in ((0, 0), (n_down, 3), (end_both, 1), (end_mixed, 2)):
+            @when(inside(j, first, first + 1))
+            def _(load=load):
+                left_loads[load].wait()
+
+        @when(inside(j, NEAR, total))
+        def _():
+            near_copy(j - NEAR).wait_send()
+
+        @when(inside(j, 0, n_down))
+        def _():
+            multiply_down(j)
+
+        @when(inside(j, n_down, end_both))
+        def _():
+            multiply_wide(j, second_t, s_both, n_down)
+
+        @when(inside(j, end_both, end_mixed))
+        def _():
+            multiply_wide(j, normed_t, s_mixed, end_both)
+
+        @when(inside(j, end_mixed, total))
+        def _():
+            multiply_wide(j, context_t, s_hidden, end_mixed)
+
+        @when(inside(j, 0, total))
+        def _():
+            pl.semaphore_wait(near_free, 1)
+            near_copy(j).start()
+
+    def stage_mid(j):
+        @when(inside(j, MID, total))
+        def _():
+            typed(j - MID, lambda kind: mid_copy(kind, j - MID).wait_send())
+
+        @when(inside(j, 0, total))
+        def _():
+            near_copy(j).wait_recv()
+            slot = j % NEAR
+            for yy in range(2):
+                value = (own_near(slot, yy)[...].astype(F32) + in_near(slot, yy)[...].astype(F32)).astype(LOW)
+
+                @pl.when(y == yy)
+                def _(value=value):
+                    cell(5, j % SUMS)[...] = value
+
+                @pl.when(y != yy)
+                def _(value=value):
+                    cell(3, j % MID)[...] = value
+
+            pl.semaphore_wait(mid_free, 1)
+
+        @when(inside(j, 0, total - NEAR))
+        def _():
+            pl.semaphore_signal(near_free, inc=1, device_id=k_mate, device_id_type=MESH)
+
+        typed(j, lambda kind: mid_copy(kind, j).start())
+
+    def stage_sum(j):
+        typed(j, lambda kind: mid_copy(kind, j).wait_recv())
+
+        @when(inside(j, 0, total))
+        def _():
+            sums = cell(5, j % SUMS)
+            sums[...] = (sums[...].astype(F32) + cell(4, j % MID)[...].astype(F32)).astype(LOW)
+
+        @when(inside(j, 0, total - MID))
+        def _():
+            pl.semaphore_signal(mid_free, inc=1, device_id=y_mate, device_id_type=MESH)
+
+    def stage_line(i, rightward):
+        free = right_free if rightward else left_free
+        for here in range(4):
+            step = here if rightward else 3 - here
+            j = i - first_z - hop * step
+            if step == 3 or (isinstance(j, int) and not 0 <= j < total):
+                continue
+
+            def device(here=here, step=step, j=j):
+                @when(inside(j, NEAR, total))
+                def _():
+                    typed(j - NEAR, lambda kind: line_copy(kind, j - NEAR, here, rightward).wait_send())
+
+                def work(kind):
+                    start, count = line_rows(kind, here, rightward)
+                    value = cell(5, j % SUMS, start, count)[...].astype(F32)
+                    if step > 0:
+                        line_copy(kind, j, here - 1 if rightward else here + 1, rightward).wait_recv()
+                        came = cell(9 if rightward else 11, j % FAR, start, count)
+                        value = value + came[...].astype(F32)
+                    cell(8, (0 if rightward else NEAR) + j % NEAR, start, count)[...] = value.astype(LOW)
+
+                typed(j, work)
+                pl.semaphore_wait(free, 1)
+                typed(j, lambda kind: line_copy(kind, j, here, rightward).start())
+
+            @pl.when(z == here)
+            def _(device=device, j=j):
+                when(inside(j, 0, total))(device)
+
+    def store(kind, j, value):
+        if kind == 0:
+            @when(inside(j, NEAR, total))
+            def _():
+                out_wait(0, j % NEAR)
+
+            piece = parts[0]
+            for t in range(3):
+                down_out[j % NEAR, t * piece : (t + 1) * piece, :] = value[:, t * 128 : (t + 1) * 128]
+            out_copy(0, j, 0).start()
+            return
+        typed(j - NEAR, lambda old: out_wait(old, j % NEAR))
+        wide_out[j % NEAR] = value
+        for first, end in ((n_down, end_both), (end_both, end_mixed), (end_mixed, total)):
+            @when(inside(j, first, end))
+            def _(first=first):
+                out_copy(1, j, first).start()
+
+    def stage_final(j):
+        if isinstance(j, int) and not 0 <= j < total:
+            return
+
+        def device(here):
+            def work(kind):
+                part = parts[kind]
+                if here == 3:
+                    line_copy(kind, j, 2, True).wait_recv()
+                if here == 0:
+                    line_copy(kind, j, 1, False).wait_recv()
+                low_at = here * part // 16 * 16
+                count = (here * part + part + 15) // 16 * 16 - low_at
+                value = cell(5, j % SUMS, low_at, count)[...].astype(F32)
+                if here > 0:
+                    value = value + cell(9, j % FAR, low_at, count)[...].astype(F32)
+                if here < 3:
+                    value = value + cell(11, j % FAR, low_at, count)[...].astype(F32)
+                shift = here * part - low_at
+                store(kind, j, value[shift : shift + part])
+
+            typed(j, work)
+
+            @when(inside(j, 0, total - FAR))
+            def _():
+                if here > 0:
+                    pl.semaphore_signal(right_free, inc=1, device_id=left, device_id_type=MESH)
+                if here < 3:
+                    pl.semaphore_signal(left_free, inc=1, device_id=right, device_id_type=MESH)
+
+        for here in range(4):
+            @pl.when(z == here)
+            def _(here=here):
+                when(inside(j, 0, total))(lambda: device(here))
+
+    def reduce_step(i):
+        stage_near(i)
+        stage_mid(i - 1)
+        stage_sum(i - 4)
+        stage_line(i, True)
+        stage_line(i, False)
+        stage_final(i - final_lag)
+
+    def reduce_steps(final, first, end):
+        @pl.when(final & (section == 0))
+        def _():
+            for i in range(first, end):
+                reduce_step(i)
+
     def norm_back(grad, source, gain, row):
         scale = column_scale(source)
         unit = source * scale
-        product = grad * unit
-        fold = product[:, :128]
-        for i in range(1, toks // 128):
-            fold = fold + product[:, i * 128 : (i + 1) * 128]
-        s_gains[row] = s_gains[row] + fold
+        folded = jnp.sum(grad * unit, axis=1, keepdims=True)
+        s_gains[:, row : row + 1] = s_gains[:, row : row + 1] + folded
         inner = grad * gain
         return scale * (inner - unit * jnp.mean(inner * unit, axis=0, keepdims=True))
 
+    def rotated_back(front, back):
+        cos, sin = cosine[...], sine[...]
+        return jnp.concatenate([front * cos + back * sin, back * cos - front * sin], axis=0)
+
+    def finish_micro(m):
+        own = at(m * toks, toks)
+
+        @pl.when(place == 0)
+        def _():
+            kv_copy(m, 0, 0, 0, 0).wait_recv()
+            kv_copy(m, 0, 1, 0, 0).wait_recv()
+            s_dkv[...] = s_dkv[...] + kv_in[m, 0].astype(F32) + kv_in[m, 1].astype(F32)
+
+        @pl.when((place == 1) | (place == 2))
+        def _():
+            kv_copy(m, 0, 0, 0, 0).wait_recv()
+            s_dkv[...] = s_dkv[...] + kv_in[m, 0].astype(F32)
+
+        for head in range(KV_HEADS):
+            front = s_dkv[head * HEAD : head * HEAD + HALF, :]
+            back = s_dkv[head * HEAD + HALF : (head + 1) * HEAD, :]
+            s_mixed[D + head * HEAD : D + (head + 1) * HEAD, own] = rotated_back(front, back).astype(LOW)
+        s_mixed[D + KVW : qkv, own] = s_dkv[KVW : 2 * KVW, :].astype(LOW)
+
+        def rest_tile(i, carry):
+            rows = at(i * TILE, TILE)
+            s_sum[rows, :] = s_sum[rows, :] + dot(v_joint[rows, D:qkv], s_mixed[D:qkv, own], 1, 0)
+            return carry
+
+        lax.fori_loop(0, D // TILE, rest_tile, 0)
+        loads(m)[5].wait()
+        g_now[...] = g_now[...] + norm_back(s_sum[...], s_x[...].astype(F32), columns[:, 0:1], 0)
+
+        @pl.when(section == 1)
+        def _():
+            g_in[m] = g_now[...].astype(LOW)
+            g_copy(m).start()
+
+        @pl.when(m + 1 < micros)
+        def _():
+            for load in loads(m + 1):
+                load.start()
+
+        @pl.when(section == 0)
+        def _():
+            copies = result_saves(m)
+            for i, save in enumerate(copies):
+                if i > 1:
+                    copies[i - 2].wait()
+                s_dq[0:toks, i % 2 * TILE : (i % 2 + 1) * TILE] = g_now[i * TILE : (i + 1) * TILE, :].T
+                save.start()
+
     def micro(m, carry):
         @pl.when(m > 0)
         def _():
-            for save in saves(m - 1):
-                save.wait()
-
             @pl.when(section == 0)
             def _():
-                result_save(m - 1).wait()
+                for save in result_saves(m - 1)[-2:]:
+                    save.wait()
+
+        @pl.when(m > 0)
+        def _():
+            for who, copy in kv_sends(m - 1):
+                @pl.when(place == who)
+                def _(copy=copy):
+                    copy.wait_send()
 
         fill_bias(bias, segments, m, place, toks)
+        own = at(m * toks, toks)
+        final = m == micros - 1
 
         @pl.when(section == 1)
         def _():
-            s_grad[...] = ends[m].astype(F32).T.astype(LOW)
+            s_grad[:, own] = ends[m].astype(F32).T.astype(LOW)
 
         @pl.when(section == 0)
         def _():
             g_copy(m).wait_recv()
-            s_grad[...] = g_in[m]
+            s_grad[:, own] = g_in[m]
 
         @pl.when(m == 0)
         def _():
             w_loads[2].wait()
 
         now = loads(m)
-        now[0].wait()
 
         def inner_tile(i, carry):
             rows, up_rows = at(i * TILE, TILE), at(FF + i * TILE, TILE)
-            grad_inner = dot(v_down[rows, :], s_grad[...], 1, 0)
-            gate, up = s_gu[rows, :], s_gu[up_rows, :]
+            for load in gu_loads(m, i):
+                load.wait()
+
+            grad_inner = dot(v_down[rows, :], s_grad[:, own], 1, 0)
+            gate, up = s_gu[i % AHEAD, 0].astype(F32), s_gu[i % AHEAD, 1].astype(F32)
             sig = jax.nn.sigmoid(gate)
-            s_both[rows, :] = (grad_inner * up * sig * (1.0 + gate * (1.0 - sig))).astype(LOW)
-            s_both[up_rows, :] = (grad_inner * (gate * sig)).astype(LOW)
+            s_both[rows, own] = (grad_inner * up * sig * (1.0 + gate * (1.0 - sig))).astype(LOW)
+            s_both[up_rows, own] = (grad_inner * (gate * sig)).astype(LOW)
+
+            @pl.when(i + AHEAD < tiles)
+            def _():
+                for load in gu_loads(m, i + AHEAD):
+                    load.start()
+
             return carry
 
-        lax.fori_loop(0, FF // TILE, inner_tile, 0)
+        lax.fori_loop(0, tiles, inner_tile, 0)
+
+        @pl.when(final)
+        def _():
+            left_loads[0].start()
+            left_loads[1].start()
 
         @pl.when(m == 0)
         def _():
@@ -1412,27 +1499,37 @@
 
         @pl.when(m + 1 < micros)
         def _():
-            loads(m + 1)[0].start()
+            for i in range(AHEAD):
+                for load in gu_loads(m + 1, i):
+                    load.start()
 
         def second_tile(i, carry):
             rows = at(i * TILE, TILE)
-            s_sum[rows, :] = dot(v_gate_up[rows, :], s_both[...], 1, 0)
+            s_sum[rows, :] = dot(v_gate_up[rows, :], s_both[:, own], 1, 0)
             return carry
 
         lax.fori_loop(0, D // TILE, second_tile, 0)
-        now[1].wait()
-        g_now[...] = s_grad[...].astype(F32) + norm_back(s_sum[...], s_hid[...], columns[:, 1:2], 1)
-        s_hidden[...] = g_now[...].astype(LOW)
+
+        @pl.when(final)
+        def _():
+            left_loads[2].start()
+            left_loads[3].start()
+            open_buffers()
+
+        now[0].wait()
+        g_now[...] = s_grad[:, own].astype(F32) + norm_back(s_sum[...], s_hid[...], columns[:, 1:2], 1)
+        s_hidden[:, own] = g_now[...].astype(LOW)
 
         @pl.when(m == 0)
         def _():
             w_loads[0].wait()
 
-        for i in (2, 3, 4, 5):
+        for i in (1, 2, 3, 4):
             now[i].wait()
+        reduce_steps(final, 0, 1)
 
         def context_tile(i, carry):
-            block = dot(v_joint[at(i * TILE, TILE), qkv:], s_hidden[...], 1, 0).astype(LOW)
+            block = dot(v_joint[at(i * TILE, TILE), qkv:], s_hidden[:, own], 1, 0).astype(LOW)
             for head in range(TILE // HEAD):
                 kv_at = i * (TILE // HEAD // GROUP) + head // GROUP
                 g = head % GROUP
@@ -1447,127 +1544,130 @@
         lax.fori_loop(0, D // TILE, context_tile, 0)
         sends = kv_sends(m)
 
-        @pl.when(place == 0)
-        def _():
-            block_grads(0, m, True)
-
-        @pl.when(place == 1)
+        reduce_steps(final, 1, 2)
+
+        @pl.when(place == 2)
         def _():
             block_grads(1, m, True)
-            kv_out[m, 0] = s_dkv[...].astype(LOW)
-            sends[0][1].start()
-            block_grads(0, m, False)
-
-        @pl.when(place == 2)
-        def _():
-            block_grads(1, m, True)
-            kv_out[m, 0] = s_dkv[...].astype(LOW)
+            kv_out[0] = s_dkv[...].astype(LOW)
             sends[1][1].start()
-            block_grads(2, m, False)
-            kv_out[m, 1] = s_dkv[...].astype(LOW)
-            sends[2][1].start()
-            block_grads(0, m, False)
 
         @pl.when(place == 3)
         def _():
             block_grads(2, m, True)
             kv_copy(m, 0, 0, 0, 3).wait_recv()
-            kv_out[m, 1] = (s_dkv[...] + kv_in[m, 0].astype(F32)).astype(LOW)
+            kv_out[1] = (s_dkv[...] + kv_in[m, 0].astype(F32)).astype(LOW)
             sends[4][1].start()
+
+        reduce_steps(final, 2, 3)
+
+        @pl.when(place == 1)
+        def _():
+            block_grads(1, m, True)
+            kv_out[0] = s_dkv[...].astype(LOW)
+            sends[0][1].start()
+
+        @pl.when(place == 2)
+        def _():
+            block_grads(2, m, False)
+            kv_out[1] = s_dkv[...].astype(LOW)
+            sends[2][1].start()
+
+        @pl.when(place == 3)
+        def _():
             block_grads(1, m, False)
-            kv_out[m, 0] = s_dkv[...].astype(LOW)
+            kv_out[0] = s_dkv[...].astype(LOW)
             sends[3][1].start()
+
+        reduce_steps(final, 3, 4)
+
+        @pl.when(place == 0)
+        def _():
+            block_grads(0, m, True)
+
+        @pl.when(place > 0)
+        def _():
             block_grads(0, m, False)
 
-        cos, sin = cosine[...], sine[...]
-
-        def rotated_back(front, back):
-            return jnp.concatenate([front * cos + back * sin, back * cos - front * sin], axis=0)
-
+        reduce_steps(final, 4, 5)
         def query_back(kv_at, carry):
             for g in range(GROUP):
                 lanes = slice(g * toks, (g + 1) * toks)
                 front = s_dq[at(kv_at * HEAD, HALF, 32), lanes] * SCALE
                 back = s_dq[at(kv_at * HEAD + HALF, HALF, 32), lanes] * SCALE
                 rows = at((kv_at * GROUP + g) * HEAD, HEAD, 64)
-                s_mixed[rows, :] = rotated_back(front, back).astype(LOW)
+                s_mixed[rows, own] = rotated_back(front, back).astype(LOW)
             return carry
 
         lax.fori_loop(0, KV_HEADS, query_back, 0)
 
         def normed_tile(i, carry):
             rows = at(i * TILE, TILE)
-            s_sum[rows, :] = dot(v_joint[rows, :D], s_mixed[:D, :], 1, 0)
+            s_sum[rows, :] = dot(v_joint[rows, :D], s_mixed[:D, own], 1, 0)
             return carry
 
         lax.fori_loop(0, D // TILE, normed_tile, 0)
-
-        @pl.when(place == 0)
-        def _():
-            kv_copy(m, 0, 0, 0, 0).wait_recv()
-            kv_copy(m, 0, 1, 0, 0).wait_recv()
-            s_dkv[...] = s_dkv[...] + kv_in[m, 0].astype(F32) + kv_in[m, 1].astype(F32)
-
-        @pl.when((place == 1) | (place == 2))
-        def _():
-            kv_copy(m, 0, 0, 0, 0).wait_recv()
-            s_dkv[...] = s_dkv[...] + kv_in[m, 0].astype(F32)
-
-        for head in range(KV_HEADS):
-            front = s_dkv[head * HEAD : head * HEAD + HALF, :]
-            back = s_dkv[head * HEAD + HALF : (head + 1) * HEAD, :]
-            s_mixed[D + head * HEAD : D + (head + 1) * HEAD, :] = rotated_back(front, back).astype(LOW)
-        s_mixed[D + KVW : qkv, :] = s_dkv[KVW : 2 * KVW, :].astype(LOW)
-
-        def rest_tile(i, carry):
-            rows = at(i * TILE, TILE)
-            s_sum[rows, :] = s_sum[rows, :] + dot(v_joint[rows, D:qkv], s_mixed[D:qkv, :], 1, 0)
-            return carry
-
-        lax.fori_loop(0, D // TILE, rest_tile, 0)
-        now[6].wait()
-        g_now[...] = g_now[...] + norm_back(s_sum[...], s_x[...].astype(F32), columns[:, 0:1], 0)
-
-        @pl.when(section == 1)
-        def _():
-            g_in[m] = g_now[...].astype(LOW)
-            g_copy(m).start()
-
-        @pl.when(m + 1 < micros)
-        def _():
-            for load in loads(m + 1)[1:]:
-                load.start()
-
-        for save in saves(m):
-            save.start()
-
-        @pl.when(section == 0)
-        def _():
-            s_result[...] = g_now[...].T
-            result_save(m).start()
+        reduce_steps(final, 5, EMBEDDED)
+
+        @pl.when((section == 1) | (m + 1 < micros))
+        def _():
+            finish_micro(m)
 
         return carry
 
     lax.fori_loop(0, micros, micro, 0)
-    gains_save = pltpu.make_async_copy(s_gains, o_gains, save_sem.at[5])
-    gains_save.start()
-    for save in saves(micros - 1):
-        save.wait()
+    def reduce_loop(i, carry):
+        reduce_step(i)
+        return carry
 
     @pl.when(section == 0)
     def _():
-        result_save(micros - 1).wait()
-
-    gains_save.wait()
+        lax.fori_loop(EMBEDDED, DEFERRED, reduce_loop, 0)
+        finish_micro(micros - 1)
+
+    rows = jnp.concatenate([s_gains[...], jnp.zeros((D, 126), F32)], axis=1).T[0:8]
+    for owner in range(OWNERS):
+        shift = (D - owner * (D // OWNERS)) % D
+        gain_out[owner] = (pltpu.roll(rows, shift, 1) if shift else rows)[:, :128]
+    for i in range(1, OWNERS):
+        gain_copy(i).start()
+
+    lax.fori_loop(jnp.where(section == 0, DEFERRED, 0), total + final_lag, reduce_loop, 0)
+    gain = gain_out[place * 4 + z]
+    for i in range(1, OWNERS):
+        gain_copy(i).wait()
+        gain = gain + gain_in[i]
+    o_gain[...] = gain
+
+    @pl.when(section == 0)
+    def _():
+        for save in result_saves(micros - 1)[-2:]:
+            save.wait()
+
     for m in range(2):
         @pl.when(section == 1)
         def _(m=m):
             g_copy(m).wait_send()
 
-        for who, copy in kv_sends(m):
-            @pl.when(place == who)
-            def _(copy=copy):
-                copy.wait_send()
+    for who, copy in kv_sends(micros - 1):
+        @pl.when(place == who)
+        def _(copy=copy):
+            copy.wait_send()
+
+    for j in range(total - NEAR, total):
+        near_copy(j).wait_send()
+        for at_z in range(3):
+            @pl.when(z == at_z)
+            def _(at_z=at_z, j=j):
+                line_copy(1, j, at_z, True).wait_send()
+
+            @pl.when(z == at_z + 1)
+            def _(at_z=at_z, j=j):
+                line_copy(1, j, at_z + 1, False).wait_send()
+    for j in range(total - MID, total):
+        mid_copy(1, j).wait_send()
+    for j in range(total - NEAR, total):
+        out_wait(1, j % NEAR)
 
 
 def run_forward(ends, gains, cosine, sine, seg_own, w_qkv, w_out, w_gate_up, w_down):
@@ -1581,14 +1681,14 @@
         ((D, micros * toks), LOW), ((D, micros * toks), LOW), ((D, micros * toks), LOW),
         ((FF, micros * toks), LOW), ((micros, D, toks), LOW), ((micros, KVW, width), LOW),
         ((micros, 3, 2 * KVW, toks), LOW), ((micros, D, toks), F32), ((micros, 8, width), F32),
-        ((micros, D, toks), F32), ((micros, 2 * FF, toks), F32), ((micros, toks, D), F32),
+        ((micros, D, toks), F32), ((micros, 2 * FF, toks), LOW), ((micros, toks, D), F32),
     ]
     scratch = [
         ((joint, D), LOW), ((2 * FF, D), LOW), ((D, FF), LOW), ((2, D, SLAB), LOW), (w_down.shape, LOW),
         ((micros, D, toks), LOW), ((D, toks), F32),
         ((D, toks), LOW), ((D, toks), LOW), ((D, toks), LOW), ((FF, toks), LOW), ((D, toks), LOW),
         ((KVW, width), LOW), ((micros, 3, 2 * KVW, toks), LOW), ((D, toks), F32), ((8, width), F32),
-        ((8, width), F32), ((D, toks), F32), ((2 * FF, toks), F32), ((toks, D), F32), ((3, toks, toks), F32),
+        ((8, width), F32), ((D, toks), F32), ((2 * FF, toks), LOW), ((toks, D), F32), ((3, toks, toks), F32),
         ((4, micros, toks), jnp.int32), ((D, 2), F32),
     ]
     return pl.pallas_call(
@@ -1610,33 +1710,38 @@
     micros, toks = ends.shape[0], ends.shape[1]
     width = GROUP * toks
     vm, hbm = pl.BlockSpec(memory_space=pltpu.VMEM), pl.BlockSpec(memory_space=pl.ANY)
-    sem = pltpu.SemaphoreType.DMA
+    sem, plain = pltpu.SemaphoreType.DMA, pltpu.SemaphoreType.REGULAR
     qkv = D + 2 * KVW
     outs = [
-        ((2 * FF, micros * toks), LOW), ((qkv, micros * toks), LOW), ((D, micros * toks), LOW),
-        ((D, micros * toks), LOW), ((2, D, 128), F32), ((micros, toks, D), F32),
+        (micros, toks, D), (FF // OWNERS, D), (D // OWNERS, 2 * FF), (D // OWNERS, qkv), (D // OWNERS, D),
+        (8, 128),
     ]
     scratch = [
         (joint.shape, LOW), (gate_up.shape, LOW), (down.shape, LOW),
         ((micros, D, toks), LOW), ((D, toks), F32),
         ((D, toks), LOW), ((KVW, width), LOW), ((3, 2 * KVW, toks), LOW), ((D, toks), F32), ((8, width), F32),
-        ((D, toks), F32), ((2 * FF, toks), F32),
-        ((2 * FF, toks), LOW), ((qkv, toks), LOW), ((D, toks), LOW), ((D, toks), LOW), ((D, toks), F32),
+        ((D, toks), F32), ((AHEAD, 2, TILE, toks), LOW),
+        ((2 * FF, micros * toks), LOW), ((qkv, micros * toks), LOW), ((D, micros * toks), LOW),
+        ((D, micros * toks), LOW), ((D, toks), F32),
         ((KVW, width), LOW), ((8, width), F32), ((KVW, width), F32), ((2 * KVW, toks), F32),
-        ((micros, 2, 2 * KVW, toks), LOW), ((micros, 2, 2 * KVW, toks), LOW),
-        ((2, D, 128), F32), ((toks, D), F32), ((3, toks, toks), F32), ((D, 2), F32),
+        ((2, 2 * KVW, toks), LOW), ((micros, 2, 2 * KVW, toks), LOW),
+        ((D, 2), F32), ((3, toks, toks), F32), ((D, 2), F32),
+        ((NEAR, D // OWNERS, WIDE_COLS), F32), ((NEAR, FF // OWNERS, DOWN_COLS), F32),
+        ((OWNERS, 8, 128), F32), ((OWNERS, 8, 128), F32),
     ]
     return pl.pallas_call(
         backward_kernel,
-        out_shape=tuple(jax.ShapeDtypeStruct(s, t) for s, t in outs),
-        in_specs=[vm] * 5 + [hbm] * 11,
-        out_specs=(hbm,) * len(outs),
+        out_shape=tuple(jax.ShapeDtypeStruct(s, F32) for s in outs),
+        in_specs=[vm] * 5 + [hbm] * 15,
+        out_specs=(hbm,) * 5 + (vm,),
         scratch_shapes=[pltpu.VMEM(s, t) for s, t in scratch]
-        + [sem((3,)), sem((7,)), sem((6,)), sem((micros, 2)), sem((micros, 2)), sem((micros,)), sem((micros,))],
+        + [sem((3,)), sem((6,)), sem((AHEAD, 2)), sem((3,)), sem((micros, 2)), sem((micros, 2)), sem((micros,)), sem((micros,))]
+        + [sem((4,)), sem((NEAR,)), sem((NEAR,)), sem((MID,)), sem((MID,)), sem((NEAR,)), sem((FAR,)), sem((NEAR,)), sem((FAR,))]
+        + [sem((NEAR,)), sem((OWNERS,)), sem((OWNERS,)), plain, plain, plain, plain],
         compiler_params=pltpu.CompilerParams(
-            collective_id=4, has_side_effects=True, vmem_limit_bytes=62 * 2**20
+            collective_id=4, has_side_effects=True, vmem_limit_bytes=63 * 2**20
         ),
-        input_output_aliases={15: 5},
+        input_output_aliases={15: 0},
         name="layer_backward",
     )(ends, gains, cosine, sine, segments, joint, gate_up, down, *saved)
 
@@ -1674,13 +1779,8 @@
     joint, gate_up, down, segments, normed, context, second, inner, *saved, result = run_forward(
         *shared, seg_local, w_qkv[0], w_out[0], w_gate_up[0], w_down[0]
     )
-    both, mixed, hidden_low, grad, gain_parts, ends_rows = run_backward(
-        *shared, segments, joint, gate_up, down, (*saved, result)
-    )
-    gain_rows = jnp.sum(gain_parts, axis=-1).reshape(2, 16, D // 16)
-    gain_tiles = jnp.pad(jnp.swapaxes(gain_rows, 0, 1), ((0, 0), (0, 6), (0, 128 - D // 16)))
-    g_down, g_gate_up, g_qkv, g_out, gain = reduce_grads(
-        (normed, context, second, inner), (both, mixed, hidden_low, grad), gain_tiles
+    ends_rows, g_down, g_gate_up, g_qkv, g_out, gain = run_backward(
+        *shared, segments, joint, gate_up, down, (*saved, result, normed, context, second, inner)
     )
     return (
         ends_rows[None, :, None], g_qkv[None], g_out[None], g_gate_up[None], g_down[None],

time: 549 us -> 534 us (0.973)
  Pallas kernels: 526 us -> 516 us
    pallas_call x1 -> x0, Pallas kernels: 175 us -> none  [reduce_grads(): pl.pallas_call(reduce_kernel, out_shape=tuple((jax.ShapeDtypeStruct(s, f3...]
    pallas_call x1, Pallas kernels: 157 us -> 323 us  [run_backward(): pl.pallas_call(backward_kernel, out_shape=tuple((jax.ShapeDtypeStruct(s,...]
where the time goes in v2:
time: 534 us; the launch traced here: 527 us
  Pallas kernels  516 us (97%)
  local copies, waits for them, and re-layouts  9.53 us (2%)
    pallas_call x1, Pallas kernels, run_backward(): pl.pallas_call(backward_kernel, out_shape=tuple((jax.ShapeDtypeStruct(s,...  323 us
    pallas_call x1, Pallas kernels, run_forward(): pl.pallas_call(forward_kernel, out_shape=tuple((jax.ShapeDtypeStruct(s, t...  193 us

profile of v2, /device:TPU:0, one launch (start us, length us, event | category | flops | bytes accessed | tf_op | source)
XLA Modules:
  0.0 527.2 jit_solution(13903381587505834971)
XLA Ops:
  0.7 1.3 copy.17
  1.9 0.8 multiply_sine_fusion
  2.7 193.3 %layer_forward.1 = (bf16[1152,3072]{1,0:T(8,128)(2,1)}, bf16[1152,6144]{1,0:T(8,128)(2,1)}, bf16[3072,1152]{1,0:T(8,128)(2,1)}, s32[4,2,256]{2,1,0:T(2,128)}, bf...) custom-call(bf16[2,256,1152]{2,1,0:T(8,128)(2,1)} %bitcast.19, ...), custom_call_target="tpu_custom_call" | custom-call | tf_op jit(solution)/shard_map/layer_forward/pallas_call | solution.py:1694
  196.1 322.6 %layer_backward.1 = (f32[2,256,1152]{2,1,0:T(8,128)}, f32[192,1152]{1,0:T(8,128)}, f32[72,6144]{1,0:T(8,128)}, f32[72,1920]{1,0:T(8,128)}, f32[72,1152]{1,0:T(8,128)}, /*index=5*/f32[8,128]{1,0:T(8,128)}) custom-call(bf16[2,256,1152]{2,1,0:T(8,128)(2,1)} %bitcast.20, f32[2,1152]{1,0:T(2,128)} %bitcast.30, ...), custom_call_target="tpu_custom_call", output_to_operand_aliasing={{0}: (15, {})} | custom-call | tf_op jit(solution)/shard_map/layer_backward/pallas_call | solution.py:1732
  518.7 1.2 slice_bitcast_fusion
  519.9 0.0 copy-start.2
  519.9 0.0 copy-start.3
  520.0 0.0 copy-start
  520.0 3.4 copy.24
  523.3 0.0 copy-done.2
  523.3 0.8 copy.25
  524.1 0.0 copy-done.3
  524.1 0.0 copy-start.1
  524.1 0.7 copy.26
  524.9 0.0 copy-done
  524.9 1.2 copy.27
  526.1 0.0 copy-done.1
  526.1 0.9 copy.28
  (2 shorter events, 0.0 us)
Async XLA Ops:
  519.9 3.4 copy-start.2
  519.9 4.2 copy-start.3
  520.0 4.9 copy-start
  524.1 1.9 copy-start.1

commit v3 on v2

--- a/solution.py
+++ b/solution.py
@@ -532,7 +532,7 @@
     first_down = JOINT_CHUNKS + WIDE_CHUNKS
     order = [(d, j) for d in (1, 2, 3) for j in range(JOINT_CHUNKS)]
     order += [(d, j) for d in (1, 2, 3) for j in range(JOINT_CHUNKS, CHUNKS)]
-    refill = {2: (3,), 3: (4,), 4: (5,), 5: (6, 7), 6: (8, 9)}
+    refill = {3: (3,), 5: (4,), 6: (5,), 7: (6, 7), 8: (8, 9)}
     done = {"relay": 0, "across": 0}
 
     def pump(upto, lag=3):
@@ -606,6 +606,11 @@
             (s_lse, o_lse.at[m]), (s_hidden, o_hidden.at[m]), (s_gu, o_gu.at[m]),
         )
         return [pltpu.make_async_copy(a, b, save_sem.at[i]) for i, (a, b) in enumerate(pairs)]
+
+    def keep(m, *items):
+        copies = saves(m)
+        for i in items:
+            copies[i].start()
 
     def result_save(m):
         return pltpu.make_async_copy(s_result, o_result.at[m], save_sem.at[11])
@@ -682,6 +687,7 @@
         x = x_now[...]
         s_x[...] = x.astype(LOW)
         s_normed[...] = (x * column_scale(x) * columns[:, 0:1]).astype(LOW)
+        keep(m, 0, 4)
         fill_bias(bias, segments, m, place, toks)
 
     def rotated(block, head):
@@ -710,6 +716,7 @@
             return carry
 
         lax.fori_loop(0, D // TILE, query_tile, 0)
+        keep(m, 5)
 
     def near_block(m):
         each(m, (0,), True)
@@ -749,6 +756,7 @@
             return carry
 
         lax.fori_loop(0, KV_HEADS, finish, 0)
+        keep(m, 1, 6, 7, 8)
 
     def seconds(m):
         def out_tile(i, carry):
@@ -761,6 +769,7 @@
         lax.fori_loop(0, D // TILE, out_tile, 0)
         hidden = s_hidden[...]
         s_second[...] = (hidden * column_scale(hidden) * columns[:, 1:2]).astype(LOW)
+        keep(m, 2, 9)
 
     def gates(first, end):
         def gate_tile(i, carry):
@@ -819,9 +828,9 @@
     early(lambda: queries(0))
     pump(joint_items + lap)
     early(lambda: near_block(0))
+    pump(joint_items + lap + 3)
+    early(lambda: far_blocks(0))
     pump(joint_items + lap + 5)
-    early(lambda: far_blocks(0))
-    pump(joint_items + lap + 6)
     early(lambda: contexts(0))
     early(lambda: seconds(0))
     pump(joint_items + 2 * lap)
@@ -887,6 +896,7 @@
             seconds(m)
             gates(0, FF // WIDE)
 
+        keep(m, 3, 10)
         for i in range(D // TILE):
             rows = slice(i * TILE, (i + 1) * TILE)
             value = s_hidden[rows, :] + dot(t_down[rows, :], s_inner[...], 1, 0)
@@ -896,9 +906,6 @@
             def _(i=i, rows=rows, value=value):
                 x_in[m, rows, :] = value.astype(LOW)
                 x_copy(m, i).start()
-
-        for save in saves(m):
-            save.start()
 
         @pl.when(section == 1)
         def _():

time: 534 us -> 517 us (0.968)
  Pallas kernels: 516 us -> 498 us
    pallas_call x1, Pallas kernels: 193 us -> 176 us  [run_forward(): pl.pallas_call(forward_kernel, out_shape=tuple((jax.ShapeDtypeStruct(s, t...]
where the time goes in v3:
time: 517 us; the launch traced here: 509 us
  Pallas kernels  498 us (96%)
  local copies, waits for them, and re-layouts  9.53 us (2%)
    pallas_call x1, Pallas kernels, run_backward(): pl.pallas_call(backward_kernel, out_shape=tuple((jax.ShapeDtypeStruct(s,...  322 us
    pallas_call x1, Pallas kernels, run_forward(): pl.pallas_call(forward_kernel, out_shape=tuple((jax.ShapeDtypeStruct(s, t...  176 us

profile of v3, /device:TPU:0, one launch (start us, length us, event | category | flops | bytes accessed | tf_op | source)
XLA Modules:
  0.0 509.3 jit_solution(11819692516853832762)
XLA Ops:
  0.7 1.3 copy.17
  1.9 0.8 multiply_sine_fusion
  2.7 176.1 %layer_forward.1 = (bf16[1152,3072]{1,0:T(8,128)(2,1)}, bf16[1152,6144]{1,0:T(8,128)(2,1)}, bf16[3072,1152]{1,0:T(8,128)(2,1)}, s32[4,2,256]{2,1,0:T(2,128)}, bf...) custom-call(bf16[2,256,1152]{2,1,0:T(8,128)(2,1)} %bitcast.19, ...), custom_call_target="tpu_custom_call" | custom-call | tf_op jit(solution)/shard_map/layer_forward/pallas_call | solution.py:1701
  178.9 321.9 %layer_backward.1 = (f32[2,256,1152]{2,1,0:T(8,128)}, f32[192,1152]{1,0:T(8,128)}, f32[72,6144]{1,0:T(8,128)}, f32[72,1920]{1,0:T(8,128)}, f32[72,1152]{1,0:T(8,128)}, /*index=5*/f32[8,128]{1,0:T(8,128)}) custom-call(bf16[2,256,1152]{2,1,0:T(8,128)(2,1)} %bitcast.20, f32[2,1152]{1,0:T(2,128)} %bitcast.30, ...), custom_call_target="tpu_custom_call", output_to_operand_aliasing={{0}: (15, {})} | custom-call | tf_op jit(solution)/shard_map/layer_backward/pallas_call | solution.py:1739
  500.8 1.2 slice_bitcast_fusion
  502.0 0.0 copy-start.2
  502.0 0.0 copy-start.3
  502.0 0.0 copy-start
  502.0 3.4 copy.24
  505.4 0.0 copy-done.2
  505.4 0.8 copy.25
  506.2 0.0 copy-done.3
  506.2 0.0 copy-start.1
  506.2 0.7 copy.26
  506.9 0.0 copy-done
  506.9 1.2 copy.27
  508.2 0.0 copy-done.1
  508.2 0.9 copy.28
  (2 shorter events, 0.0 us)
Async XLA Ops:
  502.0 3.4 copy-start.2
  502.0 4.2 copy-start.3
  502.0 4.9 copy-start
  506.2 1.9 copy-start.1

commit v4 on v3

--- a/solution.py
+++ b/solution.py
@@ -673,7 +673,7 @@
             attend(kv_at, m, blocks, fresh)
             return carry
 
-        lax.fori_loop(0, KV_HEADS, step, 0)
+        lax.fori_loop(0, KV_HEADS, step, 0, unroll=3)
 
     def take_own(m):
         x_now[...] = ends[m].astype(F32).T
@@ -1065,7 +1065,7 @@
                 s_dq[rows, :] = s_dq[rows, :] + grad_query
             return carry
 
-        lax.fori_loop(0, KV_HEADS, step, 0)
+        lax.fori_loop(0, KV_HEADS, step, 0, unroll=3)
 
     y, k = place // 2, place % 2
     y_mate = {"ctx": (1 - y) * 2 + k}

time: 517 us -> 505 us (0.977)
  Pallas kernels: 498 us -> 485 us
    pallas_call x1, Pallas kernels: 322 us -> 309 us  [run_backward(): pl.pallas_call(backward_kernel, out_shape=tuple((jax.ShapeDtypeStruct(s,...]
where the time goes in v4:
time: 505 us; the launch traced here: 497 us
  Pallas kernels  485 us (96%)
  local copies, waits for them, and re-layouts  9.53 us (2%)
    pallas_call x1, Pallas kernels, run_backward(): pl.pallas_call(backward_kernel, out_shape=tuple((jax.ShapeDtypeStruct(s,...  309 us
    pallas_call x1, Pallas kernels, run_forward(): pl.pallas_call(forward_kernel, out_shape=tuple((jax.ShapeDtypeStruct(s, t...  177 us

profile of v4, /device:TPU:0, one launch (start us, length us, event | category | flops | bytes accessed | tf_op | source)
XLA Modules:
  0.0 496.7 jit_solution(17701490559986175204)
XLA Ops:
  0.7 1.3 copy.17
  1.9 0.8 multiply_sine_fusion
  2.7 176.6 %layer_forward.1 = (bf16[1152,3072]{1,0:T(8,128)(2,1)}, bf16[1152,6144]{1,0:T(8,128)(2,1)}, bf16[3072,1152]{1,0:T(8,128)(2,1)}, s32[4,2,256]{2,1,0:T(2,128)}, bf...) custom-call(bf16[2,256,1152]{2,1,0:T(8,128)(2,1)} %bitcast.19, ...), custom_call_target="tpu_custom_call" | custom-call | tf_op jit(solution)/shard_map/layer_forward/pallas_call | solution.py:1701
  179.4 308.7 %layer_backward.1 = (f32[2,256,1152]{2,1,0:T(8,128)}, f32[192,1152]{1,0:T(8,128)}, f32[72,6144]{1,0:T(8,128)}, f32[72,1920]{1,0:T(8,128)}, f32[72,1152]{1,0:T(8,128)}, /*index=5*/f32[8,128]{1,0:T(8,128)}) custom-call(bf16[2,256,1152]{2,1,0:T(8,128)(2,1)} %bitcast.20, f32[2,1152]{1,0:T(2,128)} %bitcast.30, ...), custom_call_target="tpu_custom_call", output_to_operand_aliasing={{0}: (15, {})} | custom-call | tf_op jit(solution)/shard_map/layer_backward/pallas_call | solution.py:1739
  488.0 1.2 slice_bitcast_fusion
  489.3 0.0 copy-start.2
  489.3 0.0 copy-start.3
  489.3 0.0 copy-start
  489.3 3.4 copy.24
  492.7 0.0 copy-done.2
  492.7 0.8 copy.25
  493.5 0.0 copy-done.3
  493.5 0.0 copy-start.1
  493.5 0.7 copy.26
  494.2 0.0 copy-done
  494.2 1.2 copy.27
  495.4 0.0 copy-done.1
  495.4 0.9 copy.28
  (2 shorter events, 0.0 us)
Async XLA Ops:
  489.3 3.4 copy-start.2
  489.3 4.2 copy-start.3
  489.3 4.9 copy-start
  493.5 1.9 copy-start.1
